TPU v7x, 256 devices: a whole 4x4x8 slice. The times are simulated.
256 devices in a mesh: dp: 32 (over y_lo, z, core), mp: 8 (over x, y_hi).
Axes of the slice: x: 4, y: 4 (y_hi: 2, y_lo: 2; y = y_hi * 2 + y_lo), z: 8, core: 2. Of those that a mesh axis runs over, the one named last changes fastest.
Arguments:
- activations: bfloat16 [4096, 3584], P('dp'), may hold values from -6 to 6
- out_grads: bfloat16 [4096, 16384], P('dp', 'mp'), may hold values from -0.00390625 to 0.00390625
- slot_blocks: int32 [8, 32], replicated, may hold values from 0 to 31, as said below
- refresh_ids: int32 [8, 7], replicated, may hold values from 0 to 27, as said below
- left_stats: float32 [8, 32, 512, 512], P('mp', 'dp'), may hold values from -4 to 52, as said below
- right_stats: float32 [8, 32, 512, 512], P('mp', 'dp'), may hold values from -4 to 52, as said below
- left_roots: float32 [8, 32, 512, 512], P('mp', 'dp'), may hold values from -2 to 18, as said below
- right_roots: float32 [8, 32, 512, 512], P('mp', 'dp'), may hold values from -2 to 18, as said below
- weight_blocks: bfloat16 [8, 32, 512, 512], P('mp', 'dp'), may hold values from -0.09375 to 0.09375
Outputs:
- new_left: float32 [8, 32, 512, 512], P('mp', 'dp')
- new_right: float32 [8, 32, 512, 512], P('mp', 'dp')
- new_left_roots: float32 [8, 32, 512, 512], P('mp', 'dp')
- new_right_roots: float32 [8, 32, 512, 512], P('mp', 'dp')
- new_weights: bfloat16 [8, 32, 512, 512], P('mp', 'dp')
- projected: bfloat16 [4096, 16384], P('dp', 'mp')
Inputs may be any that keep to these rules, and one draw needn't show every extreme that they name: `slot_blocks`: each row is a permutation of 0 to 31; slot s belongs to dp index s; a value of 28 or more marks an empty slot. `refresh_ids`: each row holds 7 distinct blocks of that mp index. For every slot s and every k, at most one of the blocks held at slot s by mp indices 2 k and 2 k + 1 is listed. `left_stats`: every block is symmetric positive definite. `right_stats`: every block is symmetric positive definite. `left_roots`: every block is symmetric positive definite. `right_roots`: every block is symmetric positive definite.
All inputs are finite; a program needn't handle non-finite values.
Results may differ from a plain program's by a relative error of at most 0.0043.
Values may be sent and summed in bfloat16 or wider, within the bound.
A program may use at most 128 MiB of HBM per device.

v0:
```python
import jax
import jax.numpy as jnp
from jax import lax
from jax.sharding import PartitionSpec as P

BS = 512
FF_DEV = 2048
ITERS = 3
RB = 7
CB = 4
NBLK = 28


BETA = 0.9
STEP = 0.1
EPS = 1e-06


def mat(left, right):
    return jnp.matmul(left, right, precision=lax.Precision.HIGHEST)


def root_newton(stats):
    total = jnp.sum(stats * stats, axis=(-2, -1), keepdims=True)
    scale = 5.0 / (2.0 * jnp.sqrt(total + EPS))
    ident = jnp.eye(stats.shape[-1], dtype=jnp.float32)
    iterate = jnp.power(scale, 0.25) * ident
    coupled = scale * stats
    for step in range(ITERS):
        factor = (5.0 * ident - coupled) / 4.0
        iterate = mat(iterate, factor)
        square = mat(factor, factor)
        coupled = mat(mat(square, square), coupled)
    return iterate


def refresh_mask(block_ids, plan):
    listed = jnp.any(block_ids[:, None] == plan[None, :], axis=1)
    return listed & (block_ids < NBLK)


def column_onehot(block_ids):
    valid = block_ids < NBLK
    safe = jnp.where(valid, block_ids, 0)
    hits = (safe % CB)[:, None] == jnp.arange(CB, dtype=jnp.int32)[None, :]
    return (hits & valid[:, None]).astype(jnp.float32)


def on_device(
    activations,
    out_grads,
    slot_blocks,
    refresh_ids,
    left_stats,
    right_stats,
    left_roots,
    right_roots,
    weight_blocks,
):
    tok_rows = activations.shape[0]
    owned_count = left_stats.shape[1]
    my_mp = lax.axis_index("mp")
    my_dp = lax.axis_index("dp")
    table = lax.dynamic_index_in_dim(slot_blocks, my_mp, 0, keepdims=False)
    valid = table < NBLK
    safe = jnp.where(valid, table, 0)
    feature_blocks = activations.reshape(tok_rows, RB, BS)
    grad_blocks = out_grads.reshape(tok_rows, CB, BS)
    feat_send = jnp.take(feature_blocks, safe // CB, axis=1)
    grad_send = jnp.take(grad_blocks, safe % CB, axis=1)
    feat_recv, grad_recv = (
        lax.all_to_all(feat_send, "dp", split_axis=1, concat_axis=0, tiled=True),
        lax.all_to_all(grad_send, "dp", split_axis=1, concat_axis=0, tiled=True),
    )
    my_blocks = lax.dynamic_slice_in_dim(table, my_dp * owned_count, owned_count)
    filled = (my_blocks < NBLK).astype(jnp.float32)
    gradient = jnp.einsum("tob,toc->obc", feat_recv, grad_recv, preferred_element_type=jnp.float32)
    gradient = gradient * filled[:, None, None]
    old_left = left_stats[0]
    old_right = right_stats[0]
    old_lroot = left_roots[0]
    old_rroot = right_roots[0]
    new_left = BETA * old_left + mat(gradient, jnp.swapaxes(gradient, 1, 2))
    new_right = BETA * old_right + mat(jnp.swapaxes(gradient, 1, 2), gradient)
    update = mat(mat(old_lroot, gradient), old_rroot)
    new_weights = (weight_blocks[0].astype(jnp.float32) - STEP * update).astype(jnp.bfloat16)
    my_plan = lax.dynamic_index_in_dim(refresh_ids, my_mp, 0, keepdims=False)
    my_refresh = refresh_mask(my_blocks, my_plan)
    paired_stats = jnp.stack([new_left, new_right], axis=1)
    paired_old = jnp.stack([old_lroot, old_rroot], axis=1)

    def refresh_slot(item):
        flag, stats, previous = item
        return lax.cond(flag, lambda: root_newton(stats), lambda: previous)

    roots = lax.map(refresh_slot, (my_refresh, paired_stats, paired_old))
    new_lroot = roots[:, 0]
    new_rroot = roots[:, 1]
    piece_safe = jnp.where(table < NBLK, table, 0)
    rows_sel = jnp.take(feature_blocks, piece_safe // CB, axis=1)
    contrib = jnp.einsum(
        "tkb,kbe->tke",
        rows_sel,
        lax.all_gather(new_weights, "dp", axis=0, tiled=True),
        preferred_element_type=jnp.float32,
    )
    onehot = column_onehot(table)
    summed = jnp.einsum("tke,kc->tce", contrib, onehot, precision=lax.Precision.HIGHEST)
    projected = summed.reshape(tok_rows, FF_DEV).astype(jnp.bfloat16)
    return (
        new_left[None],
        new_right[None],
        new_lroot[None],
        new_rroot[None],
        new_weights[None],
        projected,
    )


def solution(mesh):
    in_specs = (
        P("dp", None),
        P("dp", "mp"),
        P(),
        P(),
        P("mp", "dp", None, None),
        P("mp", "dp", None, None),
        P("mp", "dp", None, None),
        P("mp", "dp", None, None),
        P("mp", "dp", None, None),
    )
    out_specs = (
        P("mp", "dp", None, None),
        P("mp", "dp", None, None),
        P("mp", "dp", None, None),
        P("mp", "dp", None, None),
        P("mp", "dp", None, None),
        P("dp", "mp"),
    )
    return jax.shard_map(
        on_device, mesh=mesh, in_specs=in_specs, out_specs=out_specs, check_vma=False
    )
```

profile of v0, /device:TPU:1, one launch (start us, length us, event | category | flops | bytes accessed | tf_op | source)
XLA Modules:
  0.0 379.9 jit_solution(15402956414772859086)
XLA Ops:
  7.2 0.7 bitcast_compare_fusion
  7.9 1.6 copy.18
  9.5 0.5 copy.19
  10.0 2.8 gather_fusion.1
  12.8 6.4 %copy.20 = bf16[32,128,512]{1,2,0:T(8,128)(2,1)} copy(bf16[32,128,512]{2,1,0:T(8,128)(2,1)} %gather_fusion.1) | data formatting | bytes 8388608 | tf_op jit(solution)/shard_map/jit(_take)/gather | solution.py:69
  19.2 4.6 %select_bitcast_fusion = bf16[128,32,512]{0,2,1:T(8,128)(2,1)} fusion(bf16[32,128,512]{1,2,0:T(8,128)(2,1)} %copy.20, pred[32]{0:T(512)(128)(4,1)S(1)} %get-tuple-element.55), kind=kLoop, calls=%fused_computation.45 | loop fusion | flops 2097152 | bytes 8388640 | tf_op jit(solution)/shard_map/jit(_take)/select_n | solution.py:69
  23.8 0.0 copy-start.7
  23.8 11.3 %all-to-all-start = ((bf16[128,32,512]{0,2,1:T(8,128)(2,1)}), bf16[128,32,512]{0,2,1:T(8,128)(2,1)}, u32[]{:S(2)}, u32[]{:S(2)}) async-start(bf16[128,32,512]{0,2,1:T(8,128)(2,1)} %select_bitcast_fusion), calls=%async_computation | async-start | bytes 8388608 | tf_op jit(solution)/shard_map/all_to_all | solution.py:72
  35.1 0.0 copy-done.7
  35.1 0.3 copy.21
  35.4 0.2 copy.22
  35.7 2.8 gather_fusion
  38.5 4.6 %select_bitcast_fusion.1 = bf16[128,32,512]{2,0,1:T(8,128)(2,1)} fusion(bf16[32,128,512]{2,1,0:T(8,128)(2,1)} %gather_fusion, pred[32]{0:T(512)(128)(4,1)S(1)} %get-tuple-element.58), kind=kLoop, calls=%fused_computation.46 | loop fusion | flops 2097152 | bytes 8388640 | tf_op jit(solution)/shard_map/jit(_take)/select_n | solution.py:70
  43.1 86.7 %all-to-all-done = bf16[128,32,512]{0,2,1:T(8,128)(2,1)} async-done(((bf16[128,32,512]{0,2,1:T(8,128)(2,1)}), bf16[128,32,512]{0,2,1:T(8,128)(2,1)}, u32[]{:S(2)}, u32[]{:S(2)}) %all-to-all-start) | async-done | bytes 4194336 | tf_op jit(solution)/shard_map/all_to_all | solution.py:72
  129.8 7.3 %all-to-all-start.1 = ((bf16[128,32,512]{2,0,1:T(8,128)(2,1)}), bf16[128,32,512]{2,0,1:T(8,128)(2,1)}, u32[]{:S(2)}, u32[]{:S(2)}) async-start(bf16[128,32,512]{2,0,1:T(8,128)(2,1)} %select_bitcast_fusion.1), calls=%async_computation.1 | async-start | bytes 8388608 | tf_op jit(solution)/shard_map/all_to_all | solution.py:73
  137.1 0.2 all-gather.3.cloned.1.call-start
  137.3 1.3 dynamic_slice.20
  139.2 92.5 %all-to-all-done.1 = bf16[128,32,512]{2,0,1:T(8,128)(2,1)} async-done(((bf16[128,32,512]{2,0,1:T(8,128)(2,1)}), bf16[128,32,512]{2,0,1:T(8,128)(2,1)}, u32[]{:S(2)}, u32[]{:S(2)}) %all-to-all-start.1) | async-done | bytes 4194336 | tf_op jit(solution)/shard_map/all_to_all | solution.py:73
  231.7 5.5 %fusion.59 = f32[512,512]{1,0:T(8,128)S(1)} fusion(bf16[128,32,512]{2,0,1:T(8,128)(2,1)} %all-to-all-done.1, bf16[128,32,512]{0,2,1:T(8,128)(2,1)} %all-to-all-done, f32[]{:T(128)} %bitcast.17), kind=kOutput, calls=%fused_computation.59 | convolution fusion | flops 2147745792 | bytes 9437188 | tf_op jit(solution)/shard_map/tob,toc->obc/dot_general | solution.py:77
  237.3 0.0 copy-done.1
  237.3 0.0 copy-start
  237.3 0.0 copy-start.8
  237.3 3.5 fusion.67
  240.8 0.0 copy-done
  240.8 0.0 copy-done.8
  240.8 0.0 copy-start.5
  240.8 2.7 fusion.65
  243.5 0.0 all-gather.3.cloned.1.call-update
  243.5 2.0 compare_reduce_fusion
  246.1 0.0 copy-done.5
  246.2 0.0 copy-start.6
  246.2 1.9 fusion.45
  248.0 0.0 copy-done.6
  248.0 0.0 copy-start.3
  248.1 0.0 copy-start.2
  248.1 1.9 fusion.51
  249.9 0.0 copy-done.3
  249.9 0.0 copy-done.2
  250.0 0.0 copy-start.4
  250.0 0.5 pad_maximum_fusion
  250.4 0.5 copy-done.4
  251.0 5.0 %conditional.1 = (f32[1,2,512,512]{3,2,1,0:T(8,128)S(1)}) conditional(s32[]{:T(128)} %bitcast.29, f32[1,2,512,512]{3,2,1,0:T(8,128)S(1)} %get-tuple-element.62, f32[1,2,512,512]{3,2,1,0:T(8,128)S(1)} %get-tuple-element.63), branch_computations={%region_1.3_spmd, %region_2.5_spmd} | conditional | flops 29000466432 | bytes 56623176 | solution.py:94
  255.9 1.5 fusion.76
  257.4 86.4 %all-gather.3.cloned.1.call-done = bf16[16384,512]{1,0:T(8,128)(2,1)} async-done(((bf16[512,512]{1,0:T(8,128)(2,1)}), bf16[16384,512]{1,0:T(8,128)(2,1)}) %all-gather.3.cloned.1.call-update) | async-done | bytes 16777232 | tf_op jit(solution)/shard_map/all_gather | solution.py:104
  343.8 11.4 %convolution_bitcast_fusion = f32[128,32,512]{0,2,1:T(8,128)} fusion(bf16[32,512,512]{2,1,0:T(8,128)(2,1)} %bitcast.124, bf16[128,32,512]{0,2,1:T(8,128)(2,1)} %select_bitcast_fusion), kind=kOutput, calls=%fused_computation.47 | convolution fusion | flops 2147483648 | bytes 29360128 | tf_op jit(solution)/shard_map/tkb,kbe->tke/dot_general | solution.py:101
  355.2 10.4 %copy.25 = f32[128,32,512]{2,1,0:T(8,128)} copy(f32[128,32,512]{0,2,1:T(8,128)} %convolution_bitcast_fusion) | data formatting | bytes 16777216 | tf_op jit(solution)/shard_map/tkb,kbe->tke/transpose | solution.py:101
  365.6 6.2 %convolution_convert_fusion = bf16[4,128,512]{2,0,1:T(4,128)(2,1)S(1)} fusion(f32[128,32,512]{2,1,0:T(8,128)} %copy.25, s32[32]{0:T(128)S(1)} %get-tuple-element.59, pred[32]{0:T(512)(128)(4,1)S(1)} %get-tuple-element.53), kind=kOutput, calls=%fused_computation.62 | convolution fusion | flops 100925696 | bytes 8913056 | tf_op jit(solution)/shard_map/tke,kc->tce/dot_general | solution.py:108
  371.9 0.9 copy.28
  (6 shorter events, 0.0 us)
Async XLA Ops:
  23.8 11.3 %copy-start.7 = (bf16[128,2048]{1,0:T(8,128)(2,1)S(1)}, bf16[128,2048]{1,0:T(8,128)(2,1)}, u32[]{:S(2)}) copy-start(bf16[128,2048]{1,0:T(8,128)(2,1)} %param.14) | copy-start | bytes 1572868
  23.8 106.0 %all-to-all-start = ((bf16[128,32,512]{0,2,1:T(8,128)(2,1)}), bf16[128,32,512]{0,2,1:T(8,128)(2,1)}, u32[]{:S(2)}, u32[]{:S(2)}) async-start(bf16[128,32,512]{0,2,1:T(8,128)(2,1)} %select_bitcast_fusion), calls=%async_computation | async-start | bytes 8388608 | tf_op jit(solution)/shard_map/all_to_all | solution.py:72
  129.8 101.9 %all-to-all-start.1 = ((bf16[128,32,512]{2,0,1:T(8,128)(2,1)}), bf16[128,32,512]{2,0,1:T(8,128)(2,1)}, u32[]{:S(2)}, u32[]{:S(2)}) async-start(bf16[128,32,512]{2,0,1:T(8,128)(2,1)} %select_bitcast_fusion.1), calls=%async_computation.1 | async-start | bytes 8388608 | tf_op jit(solution)/shard_map/all_to_all | solution.py:73
  137.1 206.7 %all-gather.3.cloned.1.call-start = ((), (), s32[]{:S(2)}) async-start(), calls=%async_computation.2 | async-start | bytes 17301504 | tf_op jit(solution)/shard_map/all_gather | solution.py:104
  231.7 5.5 %copy-start.1 = (f32[1,1,512,512]{3,2,1,0:T(8,128)S(1)}, f32[1,1,512,512]{3,2,1,0:T(8,128)}, u32[]{:S(2)}) copy-start(f32[1,1,512,512]{3,2,1,0:T(8,128)} %param.19) | copy-start | bytes 3145732
  237.3 3.5 copy-start
  237.3 3.5 copy-start.8
  240.8 5.3 %copy-start.5 = (f32[1,1,512,512]{3,2,1,0:T(8,128)S(1)}, f32[1,1,512,512]{3,2,1,0:T(8,128)}, u32[]{:S(2)}) copy-start(f32[1,1,512,512]{3,2,1,0:T(8,128)} %param.17) | copy-start | bytes 3145732
  246.2 1.9 copy-start.6
  248.0 1.9 copy-start.3
  248.1 1.9 copy-start.2
  250.0 1.0 copy-start.4
Sparse Core Ops, SparseCore 0:
  243.6 100.0 all-gather.2
where the time goes:
time: 384 us; the launch traced here: 380 us
  waiting for transfers between devices  266 us (69%)
  matrix products  33.1 us (9%)
  local copies, waits for them, and re-layouts  29.1 us (8%)
  starting transfers between devices  18.8 us (5%)
  between operations  15.9 us (4%)
  other arithmetic  12.4 us (3%)
  loops' own time  4.96 us (1%)
    all_to_all x1, waiting for transfers between devices, on_device(): lax.all_to_all(grad_send, 'dp', split_axis=1, concat_axis=0, tiled=True)  92.5 us
    all_to_all x1, waiting for transfers between devices, on_device(): lax.all_to_all(feat_send, 'dp', split_axis=1, concat_axis=0, tiled=True)  86.7 us
    all_gather x1, waiting for transfers between devices, on_device(): lax.all_gather(new_weights, 'dp', axis=0, tiled=True)  86.4 us
    dot_general x1, matrix products, on_device(): jnp.einsum('tkb,kbe->tke', rows_sel, lax.all_gather(new_weights, 'dp', ax...  11.4 us
    all_to_all x1, starting transfers between devices, on_device(): lax.all_to_all(feat_send, 'dp', split_axis=1, concat_axis=0, tiled=True)  11.3 us
    transpose x1, local copies, waits for them, and re-layouts, on_device(): jnp.einsum('tkb,kbe->tke', rows_sel, lax.all_gather(new_weights, 'dp', ax...  10.4 us
    dot_general x4, matrix products, mat(): return jnp.matmul(left, right, precision=lax.Precision.HIGHEST)  9.86 us
    gather x2, local copies, waits for them, and re-layouts, on_device(): feat_send = jnp.take(feature_blocks, safe // CB, axis=1)  9.19 us
  transfers between devices with their start and end apart: 3, of which 3 were waited for; matrix products, arithmetic and copies ran while one was open for 4% of the time, Pallas kernels for 0%

commit v1 on v0

v1 whole, which is shorter than its diff:
```python
import functools

import jax
import jax.numpy as jnp
from jax import lax
from jax.experimental import pallas as pl
from jax.experimental.pallas import tpu as pltpu
from jax.sharding import PartitionSpec as P

BETA = 0.9
STEP = 0.1
EPS = 1e-06
CB = 4

MESH = pl.DeviceIdType.MESH
BF = jnp.bfloat16
F32 = jnp.float32


def dot(left, right):
    return jnp.dot(left, right, preferred_element_type=F32)


def dot_tn(left, right):
    return lax.dot_general(left, right, (((0,), (0,)), ((), ())), preferred_element_type=F32)


def dot_nt(left, right):
    return lax.dot_general(left, right, (((1,), (1,)), ((), ())), preferred_element_type=F32)


def split(value):
    high = value.astype(BF)
    return high, (value - high.astype(F32)).astype(BF)


def kernel(
    zs, toks, rb, bs, slots,
    table, plan, act, og, ls, rs, lr, rr, wb,
    nl_out, nr_out, lroot_out, rroot_out, nw_out, proj_out,
    a_lo, a_hi, e_all, far_s, far_r, near_s, near_r, wag, acc, ysend, yrecv, pout,
    nl, nr, lold, rold, wold, lh, ll, rh, rl, gh, gl, th, tl,
    nf, m1f, xf, mb0, mb1, nb, kb, xb,
    load_sem, p0_send, p0_recv, rs_send, rs_recv, ag_send, ag_recv, sib_send, sib_recv, y_ssem, y_rsem, store_sem,
):
    half = bs // 2
    quarter = bs // 4
    far = zs // 2
    nblk = rb * CB
    dp = lax.axis_index("dp")
    mp = lax.axis_index("mp")
    core = lax.rem(dp, 2)
    z = lax.rem(dp // 2, zs)
    y = dp // (2 * zs)

    def device(yy, zz, cc):
        return yy * (2 * zs) + zz * 2 + cc

    up = lax.rem(z + 1, zs)
    down = lax.rem(z + zs - 1, zs)
    ring = ((device(y, up, core), mp), (device(y, down, core), mp))
    sibling = (device(y, z, 1 - core), mp)
    across = (device(1 - y, z, core), mp)
    across_other = (device(1 - y, z, core), mp + 1 - 2 * lax.rem(mp, 2))

    def remote(src, dst, send, recv, to):
        copy = pltpu.make_async_remote_copy(
            src_ref=src, dst_ref=dst, send_sem=send, recv_sem=recv, device_id=to, device_id_type=MESH
        )
        copy.start()
        return copy

    def rows_of(yy, cc):
        return pl.ds(pl.multiple_of((cc * 2 + yy) * toks, toks), toks)

    def local(src, dst, sem):
        copy = pltpu.make_async_copy(src, dst, sem)
        copy.start()
        return copy

    mine = rows_of(y, core)
    loads_e = [local(og.at[:, k * bs : (k + 1) * bs], e_all.at[k, mine, :], load_sem.at[k]) for k in range(CB)]
    loads_a = []
    for h, dst in enumerate((a_lo, a_hi)):
        for r in range(rb):
            lo = r * bs + h * half
            loads_a.append(local(act.at[:, lo : lo + half], dst.at[r, mine, :], load_sem.at[CB + h * rb + r]))
    base = CB + 2 * rb
    load_mats = [
        local(src, dst, load_sem.at[base + k])
        for k, (src, dst) in enumerate(((lr, lold), (rr, rold), (wb, wold), (ls, nl), (rs, nr)))
    ]

    barrier = pltpu.get_barrier_semaphore()
    for other in (sibling, across, across_other) + ring:
        pl.semaphore_signal(barrier, inc=1, device_id=other, device_id_type=MESH)
    pl.semaphore_wait(barrier, 5)

    def part(number, rows):
        if number == 0:
            return e_all.at[:, rows, :]
        if number == 1:
            return a_lo.at[:, rows, :]
        if number == 2:
            return a_hi.at[rb - 2 : rb, rows, :]
        return a_hi.at[0 : rb - 2, rows, :]

    def send_part(number, rows, slot, to):
        ref = part(number, rows)
        return remote(ref, ref, p0_send.at[slot], p0_recv.at[slot], to)

    for copy in loads_e:
        copy.wait()
    outgoing = [send_part(0, mine, 0, across)]
    own_to_sibling = [send_part(0, mine, 4, sibling)]
    for copy in loads_a:
        copy.wait()
    outgoing.append(send_part(1, mine, 1, across_other))
    own_to_sibling.append(send_part(1, mine, 5, sibling))
    outgoing.append(send_part(2, mine, 2, across))
    outgoing.append(send_part(3, mine, 3, across_other))
    own_to_sibling.append(send_part(2, mine, 6, sibling))
    own_to_sibling.append(send_part(3, mine, 7, sibling))
    theirs = rows_of(1 - y, core)
    forwarded = []
    for number in (0, 1, 2, 3):
        outgoing[number].wait_recv()
        forwarded.append(send_part(number, theirs, 8 + number, sibling))

    for copy in load_mats:
        copy.wait()
    lh[...], ll[...] = split(lold[...])
    rh[...], rl[...] = split(rold[...])

    def block_at(zz, cc):
        return table[mp, y * (2 * zs) + zz * 2 + cc]

    def row_and_col(block):
        safe = jnp.where(block < nblk, block, 0)
        return safe // CB, lax.rem(safe, CB)

    def partial_grad(zz, i):
        r, c = row_and_col(block_at(zz, core))
        return dot_tn((a_lo, a_hi)[i][r], e_all[c])

    far_copy = {}
    near_copy = {}
    for i in range(2):
        if i == 0:
            for number in (0, 1):
                own_to_sibling[number].wait_recv()
                forwarded[number].wait_recv()
        else:
            for number in (2, 3):
                own_to_sibling[number].wait_recv()
                forwarded[number].wait_recv()
        value = partial_grad(lax.rem(z + far, zs), i).astype(BF)
        for way in range(2):
            far_s[way, i] = value[:, way * half : (way + 1) * half]
            far_copy[way, i] = remote(
                far_s.at[way, i], far_r.at[way, i], rs_send.at[way, 0, i], rs_recv.at[way, 0, i], ring[way]
            )
    for d in range(far - 1, 0, -1):
        for i in range(2):
            for way in range(2):
                zz = lax.rem(z + d, zs) if way == 0 else lax.rem(z + zs - d, zs)
                value = partial_grad(zz, i)
                if d == far - 1:
                    cols = slice(way * half, (way + 1) * half)
                    rest = slice((1 - way) * half, (2 - way) * half)
                    near_s[way, d - 1, i, :, rest] = value[:, rest].astype(BF)
                    far_copy[way, i].wait_recv()
                    near_s[way, d - 1, i, :, cols] = (value[:, cols] + far_r[way, i].astype(F32)).astype(BF)
                else:
                    near_copy[way, d + 1, i].wait_recv()
                    near_s[way, d - 1, i] = (value + near_r[way, d, i].astype(F32)).astype(BF)
                near_copy[way, d, i] = remote(
                    near_s.at[way, d - 1, i],
                    near_r.at[way, d - 1, i],
                    rs_send.at[way, d, i],
                    rs_recv.at[way, d, i],
                    ring[way],
                )
    own_block = block_at(z, core)
    filled = jnp.where(own_block < nblk, 1.0, 0.0).astype(F32)
    total = None
    for i in range(2):
        rows = slice(i * half, (i + 1) * half)
        value = partial_grad(z, i)
        near_copy[0, 1, i].wait_recv()
        near_copy[1, 1, i].wait_recv()
        value = (value + near_r[0, 0, i].astype(F32) + near_r[1, 0, i].astype(F32)) * filled
        high, low = split(value)
        gh[rows, :] = high
        gl[rows, :] = low
        term = dot(lh[:, rows], high) + dot(lh[:, rows], low) + dot(ll[:, rows], high)
        total = term if total is None else total + term
    th[...], tl[...] = split(total)

    stores = []
    ag = {}
    sib = {}

    def piece(cc, zz, p, k):
        return wag.at[cc, zz, p, :, k * quarter : (k + 1) * quarter]

    def send_ring(way, zz, d, p, k):
        ref = piece(core, zz, p, k)
        ag[way, d, p, k] = remote(ref, ref, ag_send.at[way, d - 1, p, k], ag_recv.at[way, d - 1, p, k], ring[way])

    def send_sibling(zz, step, p):
        ref = wag.at[core, zz, p]
        sib[step, p] = remote(ref, ref, sib_send.at[step, p], sib_recv.at[step, p], sibling)

    def reach(way, k):
        return far if way == k else far - 1

    def behind(way, d):
        return lax.rem(z + zs - d, zs) if way == 0 else lax.rem(z + d, zs)

    def make_weights(p):
        cols = slice(p * half, (p + 1) * half)
        update = dot(th[...], rh[:, cols]) + dot(th[...], rl[:, cols]) + dot(tl[...], rh[:, cols])
        wag[core, z, p] = (wold[:, cols].astype(F32) - STEP * update).astype(BF)

    def send_own(p):
        for k in range(2):
            for way in range(2):
                order = k if way == 0 else 1 - k
                send_ring(way, z, 1, p, order)
        send_sibling(z, 0, p)
        stores.append(local(wag.at[core, z, p], nw_out.at[:, p * half : (p + 1) * half], store_sem.at[p]))

    def add_products(p, items):
        lo, hi = p * half, (p + 1) * half
        terms = []
        for cc, zz in items:
            block = block_at(zz, cc)
            r, c = row_and_col(block)
            rows = pl.ds(pl.multiple_of(core * (2 * toks), 2 * toks), 2 * toks)
            term = dot(a_lo[r, rows, :], wag[cc, zz, p, 0:half, :]) + dot(a_hi[r, rows, :], wag[cc, zz, p, half:bs, :])
            terms.append((block, c, term))
        for col in range(CB):
            value = acc[col, :, lo:hi]
            for block, c, term in terms:
                weight = jnp.where((block < nblk) & (c == col), 1.0, 0.0).astype(F32)
                value = value + term * weight
            acc[col, :, lo:hi] = value

    own_flag = jnp.zeros((), jnp.int32)
    for k in range(plan.shape[1]):
        own_flag = jnp.where(plan[mp, k] == own_block, 1, own_flag)
    own_flag = jnp.where(own_block < nblk, own_flag, 0)

    def new_left():
        nl[...] = BETA * nl[...] + dot_nt(gh[...], gh[...]) + dot_nt(gh[...], gl[...]) + dot_nt(gl[...], gh[...])
        stores.append(local(nl, nl_out, store_sem.at[2]))

    def new_right():
        nr[...] = BETA * nr[...] + dot_tn(gh[...], gh[...]) + dot_tn(gh[...], gl[...]) + dot_tn(gl[...], gh[...])
        stores.append(local(nr, nr_out, store_sem.at[3]))

    width = half

    def eye_tile(lo):
        rows = lax.broadcasted_iota(jnp.int32, (bs, width), 0)
        cols = lax.broadcasted_iota(jnp.int32, (bs, width), 1) + lo
        return jnp.where(rows == cols, 1.0, 0.0).astype(F32)

    def tiles(body):
        for lo in range(0, bs, width):
            body(slice(lo, lo + width), lo)

    def newton(stats, old, out, number):
        scale = {}

        def start():
            total = jnp.sum(stats[...] * stats[...], axis=(0, 1), keepdims=True)
            scale["z"] = 5.0 / (2.0 * jnp.sqrt(total + EPS))
            scale["root"] = jnp.sqrt(jnp.sqrt(scale["z"]))
            mb0[...] = (scale["z"] * stats[...]).astype(BF)

            def body(cols, lo):
                value = (-0.625 * scale["z"]) * stats[:, cols] + 0.0625 * dot(mb0[...], mb0[:, cols])
                nf[:, cols] = value
                nb[:, cols] = value.astype(BF)

            tiles(body)

        def fourth_power():
            def body(cols, lo):
                kb[:, cols] = (3.125 * nf[:, cols] + dot(nb[...], nb[:, cols])).astype(BF)

            tiles(body)

        def first_coupled():
            def body(cols, lo):
                value = (2.44140625 * scale["z"]) * stats[:, cols] + dot(kb[...], mb0[:, cols])
                m1f[:, cols] = value
                mb1[:, cols] = value.astype(BF)

            tiles(body)

        def second_iterate():
            def body(cols, lo):
                value = 1.5625 * eye_tile(lo) - 0.3125 * (scale["z"] * stats[:, cols] + m1f[:, cols])
                value = scale["root"] * (value + 0.0625 * dot(mb0[...], mb1[:, cols]))
                xf[:, cols] = value
                xb[:, cols] = value.astype(BF)

            tiles(body)

        def second_square():
            def body(cols, lo):
                value = -0.625 * m1f[:, cols] + 0.0625 * dot(mb1[...], mb1[:, cols])
                nf[:, cols] = value
                nb[:, cols] = value.astype(BF)

            tiles(body)

        def second_coupled():
            def body(cols, lo):
                mb0[:, cols] = (2.44140625 * m1f[:, cols] + dot(kb[...], mb1[:, cols])).astype(BF)

            tiles(body)

        def finish():
            mask = jnp.full((bs, width), own_flag, jnp.int32) > 0

            def body(cols, lo):
                value = 1.25 * xf[:, cols] - 0.25 * dot(xb[...], mb0[:, cols])
                old[:, cols] = jnp.where(mask, value, old[:, cols])

            tiles(body)
            stores.append(local(old, out, store_sem.at[number]))

        return [start, fourth_power, first_coupled, second_iterate, second_square, fourth_power, second_coupled, finish]

    work = [new_left, new_right] + newton(nl, lold, lroot_out, 4) + newton(nr, rold, rroot_out, 5)

    def some(count):
        for _ in range(count):
            if work:
                work.pop(0)()

    def projection_part(p):
        other = pl.ds(pl.multiple_of((1 - y) * toks, toks), toks)
        ysend[p] = acc[:, other, p * half : (p + 1) * half].astype(BF)
        return remote(ysend.at[p], yrecv.at[p], y_ssem.at[p], y_rsem.at[p], across)

    def projection_end(p, copy):
        copy.wait_recv()
        own = pl.ds(pl.multiple_of(y * toks, toks), toks)
        value = acc[:, own, p * half : (p + 1) * half] + yrecv[p].astype(F32)
        for col in range(CB):
            lo = col * bs + p * half
            pout[:, lo : lo + half] = value[col].astype(BF)

    make_weights(0)
    send_own(0)
    make_weights(1)
    acc[...] = jnp.zeros_like(acc)
    some(2)
    y_copy = {}
    steps = 2 * zs - 2
    for p in range(2):
        if p == 1:
            add_products(1, [(core, z)])
        else:
            add_products(0, [(core, z)])
        sib_step = 1
        pending = [(0, z)]
        for d in range(1, far + 1):
            arrived = []
            for k in range(2):
                for way in range(2):
                    order = k if way == 0 else 1 - k
                    if d <= reach(way, order):
                        ag[way, d, p, order].wait_recv()
                        if d < reach(way, order):
                            send_ring(way, behind(way, d), d + 1, p, order)
            if d < far:
                arrived = [behind(0, d), behind(1, d)]
            else:
                arrived = [behind(0, d)]
            fresh = []
            for zz in arrived:
                send_sibling(zz, sib_step, p)
                fresh.append((sib_step, zz))
                sib_step += 1
            if p == 0 and d == far - 1:
                send_own(1)
            some(2 if p == 0 else 3)
            items = [(core, zz) for zz in arrived]
            for step, zz in pending:
                sib[step, p].wait_recv()
                items.append((1 - core, zz))
            add_products(p, items)
            pending = fresh
        items = []
        for step, zz in pending:
            sib[step, p].wait_recv()
            items.append((1 - core, zz))
        add_products(p, items)
        y_copy[p] = projection_part(p)
    some(len(work))
    for p in range(2):
        projection_end(p, y_copy[p])
    stores.append(local(pout, proj_out, store_sem.at[6]))

    for copy in outgoing + own_to_sibling + forwarded:
        copy.wait_send()
    for group in (far_copy, near_copy, ag, sib, y_copy):
        for copy in group.values():
            copy.wait_send()
    for copy in stores:
        copy.wait()


def solution(mesh):
    zs = mesh.shape["dp"] // 4

    def on_device(act, og, table, plan, ls, rs, lr, rr, wb):
        toks = act.shape[0]
        bs = ls.shape[-1]
        rb = act.shape[1] // bs
        slots = table.shape[1]
        half = bs // 2
        mats = [value.reshape(bs, bs) for value in (ls, rs, lr, rr, wb)]
        far = zs // 2
        square = jax.ShapeDtypeStruct((bs, bs), F32)
        any_space = pl.BlockSpec(memory_space=pl.ANY)
        smem = pl.BlockSpec(memory_space=pltpu.SMEM)
        f_mat = pltpu.VMEM((bs, bs), F32)
        b_mat = pltpu.VMEM((bs, bs), BF)
        dma = pltpu.SemaphoreType.DMA
        outs = pl.pallas_call(
            functools.partial(kernel, zs, toks, rb, bs, slots),
            out_shape=[
                square,
                square,
                square,
                square,
                jax.ShapeDtypeStruct((bs, bs), BF),
                jax.ShapeDtypeStruct((toks, CB * bs), BF),
            ],
            in_specs=[smem, smem] + [any_space] * 7,
            out_specs=[any_space] * 6,
            scratch_shapes=[
                pltpu.VMEM((rb, 4 * toks, half), BF),
                pltpu.VMEM((rb, 4 * toks, half), BF),
                pltpu.VMEM((CB, 4 * toks, bs), BF),
                pltpu.VMEM((2, 2, half, half), BF),
                pltpu.VMEM((2, 2, half, half), BF),
                pltpu.VMEM((2, far - 1, 2, half, bs), BF),
                pltpu.VMEM((2, far - 1, 2, half, bs), BF),
                pltpu.VMEM((2, zs, 2, bs, half), BF),
                pltpu.VMEM((CB, 2 * toks, bs), F32),
                pltpu.VMEM((2, CB, toks, half), BF),
                pltpu.VMEM((2, CB, toks, half), BF),
                pltpu.VMEM((toks, CB * bs), BF),
                f_mat, f_mat, f_mat, f_mat, b_mat,
                b_mat, b_mat, b_mat, b_mat, b_mat, b_mat, b_mat, b_mat,
                f_mat, f_mat, f_mat, b_mat, b_mat, b_mat, b_mat, b_mat,
                dma((CB + 2 * rb + 5,)),
                dma((12,)), dma((12,)),
                dma((2, far, 2)), dma((2, far, 2)),
                dma((2, far, 2, 2)), dma((2, far, 2, 2)),
                dma((zs, 2)), dma((zs, 2)),
                dma((2,)), dma((2,)),
                dma((7,)),
            ],
            compiler_params=pltpu.CompilerParams(
                collective_id=0, has_side_effects=True, vmem_limit_bytes=56 * 1024 * 1024
            ),
        )(table, plan, act, og, *mats)
        return tuple(value.reshape(1, 1, bs, bs) for value in outs[:5]) + (outs[5],)

    block = P("mp", "dp", None, None)
    return jax.shard_map(
        on_device,
        mesh=mesh,
        in_specs=(P("dp", None), P("dp", "mp"), P(), P(), block, block, block, block, block),
        out_specs=(block, block, block, block, block, P("dp", "mp")),
        check_vma=False,
    )
```

time: 384 us -> 135 us (0.35)
  waiting for transfers between devices: 266 us -> 0 us
  Pallas kernels: 0 us -> 125 us
  matrix products: 33.1 us -> 0 us
  local copies, waits for them, and re-layouts: 29.1 us -> 8.98 us
  starting transfers between devices: 18.8 us -> 0 us
  between operations: 15.9 us -> 0.66 us
  other arithmetic: 12.4 us -> 0 us
  loops' own time: 4.96 us -> 0 us
    all_to_all x2 -> x0, waiting for transfers between devices: 179 us -> none  [the longest x1 92.5 us: on_device(): lax.all_to_all(grad_send, 'dp', split_axis=1, concat_axis=0, tiled=True)]
    pallas_call x0 -> x1, Pallas kernels: none -> 125 us  [on_device(): pl.pallas_call(functools.partial(kernel, zs, toks, rb, bs, slots), out_sh...]
    all_gather x1 -> x0, waiting for transfers between devices: 86.4 us -> none  [on_device(): lax.all_gather(new_weights, 'dp', axis=0, tiled=True)]
    dot_general x7 -> x0, matrix products: 33.1 us -> none  [the longest x1 11.4 us: on_device(): jnp.einsum('tkb,kbe->tke', rows_sel, lax.all_gather(new_weights, 'dp', ax...]
    all_to_all x2 -> x0, starting transfers between devices: 18.6 us -> none  [the longest x1 11.3 us: on_device(): lax.all_to_all(feat_send, 'dp', split_axis=1, concat_axis=0, tiled=True)]
    gather x3 -> x0, local copies, waits for them, and re-layouts: 12 us -> none  [the longest x2 9.19 us: on_device(): feat_send = jnp.take(feature_blocks, safe // CB, axis=1)]
    transpose x1 -> x0, local copies, waits for them, and re-layouts: 10.4 us -> none  [on_device(): jnp.einsum('tkb,kbe->tke', rows_sel, lax.all_gather(new_weights, 'dp', ax...]
    select_n x3 -> x0, other arithmetic: 9.26 us -> none  [the longest x2 4.64 us: on_device(): grad_send = jnp.take(grad_blocks, safe % CB, axis=1)]
  transfers between devices with their start and end apart: 3 -> 0, of which waited for: 3 -> 0; matrix products, arithmetic and copies ran while one was open for 4% -> 0% of each run, Pallas kernels for 0% -> 0%
where the time goes in v1:
time: 135 us
  Pallas kernels  125 us (93%)
  local copies, waits for them, and re-layouts  8.98 us (7%)
    pallas_call x1, Pallas kernels, on_device(): pl.pallas_call(functools.partial(kernel, zs, toks, rb, bs, slots), out_sh...  125 us
    unnamed x16, local copies, waits for them, and re-layouts  8.98 us

profile of v1, /device:TPU:1, one launch (start us, length us, event | category | flops | bytes accessed | tf_op | source)
XLA Modules:
  0.0 134.6 jit_solution(4918445960311660862)
XLA Ops:
  0.6 125.0 %shard_map.136 = (f32[512,512]{1,0:T(8,128)}, f32[512,512]{1,0:T(8,128)}, f32[512,512]{1,0:T(8,128)}, f32[512,512]{1,0:T(8,128)}, bf16[512,512]{1,0:T(8,128)(2,1)}, /*index=5*/bf16[128,2048]{1,0:T(8,128)(2,1)}) custom-call(s32[8,32]{1,0:T(8,128)} %table.1, s32[8,7]{1,0:T(8,128)} %plan.1, bf16[128,3584]{1,0:T(8,128)(2,1)} %act.1, bf16[128,2048]{1,0:T(8,128)(2,1)} %og.1, ...), custom_call_target="tpu_custom_call" | custom-call | tf_op jit(solution)/shard_map/pallas_call | solution.py:437
  125.6 0.0 copy-start.2
  125.6 2.4 %copy.21 = f32[1,1,512,512]{3,2,1,0:T(8,128)} copy(f32[1,1,512,512]{3,2,1,0:T(8,128)} %bitcast.13) | data formatting | bytes 2097152
  128.0 0.0 copy-done.2
  128.0 0.0 copy-start.1
  128.0 1.0 copy.22
  129.0 0.6 copy-done.1
  129.6 0.0 copy-start
  129.6 1.0 copy.23
  130.6 0.6 copy-done
  131.2 0.0 copy-start.4
  131.2 1.0 copy.24
  132.2 0.4 copy-done.4
  132.6 0.0 copy-start.3
  132.6 0.8 copy.25
  133.4 0.4 copy-done.3
  133.8 0.8 copy.26
Async XLA Ops:
  125.6 2.4 %copy-start.2 = (f32[512,512]{1,0:T(8,128)S(1)}, f32[512,512]{1,0:T(8,128)}, u32[]{:S(2)}) copy-start(f32[512,512]{1,0:T(8,128)} %get-tuple-element.13) | copy-start | bytes 3145732
  128.0 1.6 %copy-start.1 = (f32[512,512]{1,0:T(8,128)S(1)}, f32[512,512]{1,0:T(8,128)}, u32[]{:S(2)}) copy-start(f32[512,512]{1,0:T(8,128)} %get-tuple-element.14) | copy-start | bytes 3145732
  129.6 1.6 %copy-start = (f32[512,512]{1,0:T(8,128)S(1)}, f32[512,512]{1,0:T(8,128)}, u32[]{:S(2)}) copy-start(f32[512,512]{1,0:T(8,128)} %get-tuple-element.15) | copy-start | bytes 3145732
  131.2 1.4 %copy-start.4 = (bf16[512,512]{1,0:T(8,128)(2,1)S(1)}, bf16[512,512]{1,0:T(8,128)(2,1)}, u32[]{:S(2)}) copy-start(bf16[512,512]{1,0:T(8,128)(2,1)} %get-tuple-element.16) | copy-start | bytes 1572868
  132.6 1.2 copy-start.3

commit v2 on v1

v2 whole, which is shorter than its diff:
```python
import functools

import jax
import jax.numpy as jnp
from jax import lax
from jax.experimental import pallas as pl
from jax.experimental.pallas import tpu as pltpu
from jax.sharding import PartitionSpec as P

BETA = 0.9
STEP = 0.1
EPS = 1e-06
CB = 4

STAGGER = False
LAG = 1

MESH = pl.DeviceIdType.MESH
BF = jnp.bfloat16
F32 = jnp.float32


def dot(left, right):
    return jnp.dot(left, right, preferred_element_type=F32)


def dot_tn(left, right):
    return lax.dot_general(left, right, (((0,), (0,)), ((), ())), preferred_element_type=F32)


def dot_nt(left, right):
    return lax.dot_general(left, right, (((1,), (1,)), ((), ())), preferred_element_type=F32)


def split(value):
    high = value.astype(BF)
    return high, (value - high.astype(F32)).astype(BF)


def kernel(
    zs, toks, rb, bs, slots,
    table, plan, act, og, ls, rs, lr, rr, wb,
    nl, nr, lold, rold, nw, pout,
    a_lo, a_hi, e_lo, e_hi, far_s, far_r, near_s, near_r, wag, acc, ysend, yrecv,
    wold, lh, ll, rh, rl, gh, gl, th, tl, tf,
    nf, m1f, xf, mb0, mb1, nb, kb, xb,
    gate, load_sem, p0_send, p0_recv, rs_send, rs_recv, ag_send, ag_recv, sib_send, sib_recv, y_ssem, y_rsem,
):
    half = bs // 2
    quarter = bs // 4
    far = zs // 2
    nblk = rb * CB
    dp = lax.axis_index("dp")
    mp = lax.axis_index("mp")
    core = lax.rem(dp, 2)
    z = lax.rem(dp // 2, zs)
    y = dp // (2 * zs)

    def device(yy, zz, cc):
        return yy * (2 * zs) + zz * 2 + cc

    up = lax.rem(z + 1, zs)
    down = lax.rem(z + zs - 1, zs)
    ring = ((device(y, up, core), mp), (device(y, down, core), mp))
    sibling = (device(y, z, 1 - core), mp)
    across = (device(1 - y, z, core), mp)
    across_other = (device(1 - y, z, core), mp + 1 - 2 * lax.rem(mp, 2))

    def remote(src, dst, send, recv, to):
        copy = pltpu.make_async_remote_copy(
            src_ref=src, dst_ref=dst, send_sem=send, recv_sem=recv, device_id=to, device_id_type=MESH
        )
        copy.start()
        return copy

    def rows_of(yy, cc):
        return pl.ds(pl.multiple_of((cc * 2 + yy) * toks, toks), toks)

    def local(src, dst, sem):
        copy = pltpu.make_async_copy(src, dst, sem)
        copy.start()
        return copy

    mine = rows_of(y, core)
    loads = {}
    for h, (e_dst, a_dst) in enumerate(((e_lo, a_lo), (e_hi, a_hi))):
        first = h * (CB + rb)
        loads["e", h] = [
            local(og.at[:, k * bs + h * half : k * bs + (h + 1) * half], e_dst.at[k, mine, :], load_sem.at[first + k])
            for k in range(CB)
        ]
        loads["a", h] = [
            local(act.at[:, r * bs + h * half : r * bs + (h + 1) * half], a_dst.at[r, mine, :], load_sem.at[first + CB + r])
            for r in range(rb)
        ]
    base = 2 * (CB + rb)
    load_mats = [
        local(src, dst, load_sem.at[base + k])
        for k, (src, dst) in enumerate(((lr, lold), (rr, rold), (wb, wold), (ls, nl), (rs, nr)))
    ]

    barrier = pltpu.get_barrier_semaphore()
    for other in (sibling, across, across_other) + ring:
        pl.semaphore_signal(barrier, inc=1, device_id=other, device_id_type=MESH)
    pl.semaphore_wait(barrier, 5)

    def part(number, rows):
        return (
            e_lo.at[:, rows, :],
            a_lo.at[rb - 2 : rb, rows, :],
            a_lo.at[0 : rb - 2, rows, :],
            e_hi.at[:, rows, :],
            a_hi.at[rb - 1 : rb, rows, :],
            a_hi.at[0 : rb - 1, rows, :],
        )[number]

    parts = 6

    def send_part(number, rows, slot, to):
        ref = part(number, rows)
        return remote(ref, ref, p0_send.at[slot], p0_recv.at[slot], to)

    outgoing = {}
    to_sibling = {}
    forwarded = {}
    for what, numbers in ((("e", 0), (0,)), (("a", 0), (1, 2)), (("e", 1), (3,)), (("a", 1), (4, 5))):
        for copy in loads[what]:
            copy.wait()
        if numbers == (3,):
            for number in (0, 1, 2):
                outgoing[number].wait_send()
        for number in numbers:
            to = across_other if number in (2, 5) else across
            outgoing[number] = send_part(number, mine, number, to)
            to_sibling[number] = send_part(number, mine, parts + number, sibling)
    theirs = rows_of(1 - y, core)

    def forward(numbers):
        for number in numbers:
            outgoing[number].wait_recv()
            forwarded[number] = send_part(number, theirs, 2 * parts + number, sibling)

    def have(numbers):
        for number in numbers:
            to_sibling[number].wait_recv()
            forwarded[number].wait_recv()

    def block_at(zz, cc):
        return table[mp, y * (2 * zs) + zz * 2 + cc]

    def row_and_col(block):
        safe = jnp.where(block < nblk, block, 0)
        return safe // CB, lax.rem(safe, CB)

    def partial_grad(zz, i, j):
        r, c = row_and_col(block_at(zz, core))
        return dot_tn((a_lo, a_hi)[i][r], (e_lo, e_hi)[j][c])

    far_copy = {}
    near_copy = {}

    def send_far(i, j):
        value = partial_grad(lax.rem(z + far, zs), i, j).astype(BF)
        for way in range(2):
            far_s[way, i, j] = value[way * quarter : (way + 1) * quarter, :]
            far_copy[way, i, j] = remote(
                far_s.at[way, i, j], far_r.at[way, i, j], rs_send.at[way, 0, i, j], rs_recv.at[way, 0, i, j], ring[way]
            )

    def send_near(d, i, j):
        for way in range(2):
            zz = lax.rem(z + d, zs) if way == 0 else lax.rem(z + zs - d, zs)
            value = partial_grad(zz, i, j)
            if d == far - 1:
                rows = slice(way * quarter, (way + 1) * quarter)
                rest = slice((1 - way) * quarter, (2 - way) * quarter)
                near_s[way, d - 1, i, j, rest, :] = value[rest, :].astype(BF)
                far_copy[way, i, j].wait_recv()
                near_s[way, d - 1, i, j, rows, :] = (value[rows, :] + far_r[way, i, j].astype(F32)).astype(BF)
            else:
                near_copy[way, d + 1, i, j].wait_recv()
                near_s[way, d - 1, i, j] = (value + near_r[way, d, i, j].astype(F32)).astype(BF)
            near_copy[way, d, i, j] = remote(
                near_s.at[way, d - 1, i, j],
                near_r.at[way, d - 1, i, j],
                rs_send.at[way, d, i, j],
                rs_recv.at[way, d, i, j],
                ring[way],
            )

    forward((0, 1, 2))
    have((0, 1, 2))
    if STAGGER:

        @pl.when(core == 1)
        def _():
            pl.semaphore_wait(gate, 1)

    send_far(0, 0)
    send_near(far - 1, 0, 0)
    if STAGGER:

        @pl.when(core == 0)
        def _():
            pl.semaphore_signal(gate, inc=1, device_id=sibling, device_id_type=MESH)

    forward((3,))
    have((3,))
    send_far(0, 1)
    send_near(far - 1, 0, 1)
    forward((4, 5))
    have((4, 5))
    send_far(1, 0)
    send_far(1, 1)
    for copy in load_mats:
        copy.wait()
    lh[...], ll[...] = split(lold[...])
    rh[...], rl[...] = split(rold[...])
    quarters = ((0, 0), (0, 1), (1, 0), (1, 1))
    order = sorted((2 * (far - 1 - d) + (0, 0.6, 1.1, 1.6)[n], d, q) for d in range(far - 1, 0, -1) for n, q in enumerate(quarters))
    for _, d, (i, j) in order:
        if (d, i, j) not in ((far - 1, 0, 0), (far - 1, 0, 1)):
            send_near(d, i, j)
    own_block = block_at(z, core)
    filled = jnp.where(own_block < nblk, 1.0, 0.0).astype(F32)
    lefts = [None, None]
    for i, j in quarters:
        rows = slice(i * half, (i + 1) * half)
        cols = slice(j * half, (j + 1) * half)
        value = partial_grad(z, i, j)
        near_copy[0, 1, i, j].wait_recv()
        near_copy[1, 1, i, j].wait_recv()
        value = (value + near_r[0, 0, i, j].astype(F32) + near_r[1, 0, i, j].astype(F32)) * filled
        high, low = split(value)
        gh[rows, cols] = high
        gl[rows, cols] = low
        term = dot(lh[:, rows], high) + dot(lh[:, rows], low) + dot(ll[:, rows], high)
        lefts[j] = term if i == 0 else lefts[j] + term
        if i == 1:
            th[:, cols], tl[:, cols] = split(lefts[j])
            if j == 0:
                tf[...] = dot(th[:, cols], rh[cols, 0:half]) + dot(th[:, cols], rl[cols, 0:half]) + dot(tl[:, cols], rh[cols, 0:half])

    ag = {}
    sib = {}

    def piece(cc, zz, p, k):
        return wag.at[cc, zz, p, :, k * quarter : (k + 1) * quarter]

    def send_ring(way, zz, d, p, k):
        ref = piece(core, zz, p, k)
        ag[way, d, p, k] = remote(ref, ref, ag_send.at[way, d - 1, p, k], ag_recv.at[way, d - 1, p, k], ring[way])

    def send_sibling(zz, step, p):
        ref = wag.at[core, zz, p]
        sib[step, p] = remote(ref, ref, sib_send.at[step, p], sib_recv.at[step, p], sibling)

    def reach(way, k):
        return far if way == k else far - 1

    def behind(way, d):
        return lax.rem(z + zs - d, zs) if way == 0 else lax.rem(z + d, zs)

    def make_weights(p):
        cols = slice(p * half, (p + 1) * half)
        if p == 0:
            rows = slice(half, bs)
            update = tf[...]
        else:
            rows = slice(0, bs)
            update = 0.0
        update += dot(th[:, rows], rh[rows, cols]) + dot(th[:, rows], rl[rows, cols]) + dot(tl[:, rows], rh[rows, cols])
        value = (wold[:, cols].astype(F32) - STEP * update).astype(BF)
        wag[core, z, p] = value
        nw[:, cols] = value

    def send_own(p):
        for k in range(2):
            for way in range(2):
                order = k if way == 0 else 1 - k
                send_ring(way, z, 1, p, order)
        send_sibling(z, 0, p)

    def add_products(p, items):
        lo, hi = p * half, (p + 1) * half
        terms = []
        for cc, zz in items:
            block = block_at(zz, cc)
            r, c = row_and_col(block)
            rows = pl.ds(pl.multiple_of(core * (2 * toks), 2 * toks), 2 * toks)
            term = dot(a_lo[r, rows, :], wag[cc, zz, p, 0:half, :]) + dot(a_hi[r, rows, :], wag[cc, zz, p, half:bs, :])
            terms.append((block, c, term))
        for col in range(CB):
            value = acc[col, :, lo:hi]
            for block, c, term in terms:
                weight = jnp.where((block < nblk) & (c == col), 1.0, 0.0).astype(F32)
                value = value + term * weight
            acc[col, :, lo:hi] = value

    own_flag = jnp.zeros((), jnp.int32)
    for k in range(plan.shape[1]):
        own_flag = jnp.where(plan[mp, k] == own_block, 1, own_flag)
    own_flag = jnp.where(own_block < nblk, own_flag, 0)

    def new_left():
        nl[...] = BETA * nl[...] + dot_nt(gh[...], gh[...]) + dot_nt(gh[...], gl[...]) + dot_nt(gl[...], gh[...])

    def new_right():
        nr[...] = BETA * nr[...] + dot_tn(gh[...], gh[...]) + dot_tn(gh[...], gl[...]) + dot_tn(gl[...], gh[...])

    width = half

    def eye_tile(lo):
        rows = lax.broadcasted_iota(jnp.int32, (bs, width), 0)
        cols = lax.broadcasted_iota(jnp.int32, (bs, width), 1) + lo
        return jnp.where(rows == cols, 1.0, 0.0).astype(F32)

    def tiles(body):
        for lo in range(0, bs, width):
            body(slice(lo, lo + width), lo)

    def newton(stats, old):
        scale = {}

        def start():
            total = jnp.sum(stats[...] * stats[...], axis=(0, 1), keepdims=True)
            scale["z"] = 5.0 / (2.0 * jnp.sqrt(total + EPS))
            scale["root"] = jnp.sqrt(jnp.sqrt(scale["z"]))
            mb0[...] = (scale["z"] * stats[...]).astype(BF)

            def body(cols, lo):
                value = (-0.625 * scale["z"]) * stats[:, cols] + 0.0625 * dot(mb0[...], mb0[:, cols])
                nf[:, cols] = value
                nb[:, cols] = value.astype(BF)

            tiles(body)

        def fourth_power():
            def body(cols, lo):
                kb[:, cols] = (3.125 * nf[:, cols] + dot(nb[...], nb[:, cols])).astype(BF)

            tiles(body)

        def first_coupled():
            def body(cols, lo):
                value = (2.44140625 * scale["z"]) * stats[:, cols] + dot(kb[...], mb0[:, cols])
                m1f[:, cols] = value
                mb1[:, cols] = value.astype(BF)

            tiles(body)

        def second_iterate():
            def body(cols, lo):
                value = 1.5625 * eye_tile(lo) - 0.3125 * (scale["z"] * stats[:, cols] + m1f[:, cols])
                value = scale["root"] * (value + 0.0625 * dot(mb0[...], mb1[:, cols]))
                xf[:, cols] = value
                xb[:, cols] = value.astype(BF)

            tiles(body)

        def second_square():
            def body(cols, lo):
                value = -0.625 * m1f[:, cols] + 0.0625 * dot(mb1[...], mb1[:, cols])
                nf[:, cols] = value
                nb[:, cols] = value.astype(BF)

            tiles(body)

        def second_coupled():
            def body(cols, lo):
                mb0[:, cols] = (2.44140625 * m1f[:, cols] + dot(kb[...], mb1[:, cols])).astype(BF)

            tiles(body)

        def finish():
            mask = jnp.full((bs, width), own_flag, jnp.int32) > 0

            def body(cols, lo):
                value = 1.25 * xf[:, cols] - 0.25 * dot(xb[...], mb0[:, cols])
                old[:, cols] = jnp.where(mask, value, old[:, cols])

            tiles(body)

        return [start, fourth_power, first_coupled, second_iterate, second_square, fourth_power, second_coupled, finish]

    work = [new_left, new_right] + newton(nl, lold) + newton(nr, rold)

    def some(count):
        for _ in range(count):
            if work:
                work.pop(0)()

    def projection_part(p):
        other = pl.ds(pl.multiple_of((1 - y) * toks, toks), toks)
        ysend[p] = acc[:, other, p * half : (p + 1) * half].astype(BF)
        return remote(ysend.at[p], yrecv.at[p], y_ssem.at[p], y_rsem.at[p], across)

    def projection_end(p, copy):
        copy.wait_recv()
        own = pl.ds(pl.multiple_of(y * toks, toks), toks)
        value = acc[:, own, p * half : (p + 1) * half] + yrecv[p].astype(F32)
        for col in range(CB):
            lo = col * bs + p * half
            pout[:, lo : lo + half] = value[col].astype(BF)

    make_weights(0)
    send_own(0)
    make_weights(1)
    acc[...] = jnp.zeros_like(acc)
    some(2)
    y_copy = {}
    for p in range(2):
        if p == 1:
            add_products(1, [(core, z)])
        else:
            add_products(0, [(core, z)])
        sib_step = 1
        pending = [[(0, z)]]
        for d in range(1, far + 1):
            for k in range(2):
                for way in range(2):
                    order = k if way == 0 else 1 - k
                    if d <= reach(way, order):
                        ag[way, d, p, order].wait_recv()
                        if d < reach(way, order):
                            send_ring(way, behind(way, d), d + 1, p, order)
            arrived = [behind(0, d), behind(1, d)] if d < far else [behind(0, d)]
            fresh = []
            for zz in arrived:
                send_sibling(zz, sib_step, p)
                fresh.append((sib_step, zz))
                sib_step += 1
            pending.append(fresh)
            if p == 0 and d == far - 1:
                send_own(1)
            some(2 if p == 0 else 3)
            items = [(core, zz) for zz in arrived]
            if len(pending) > LAG:
                for step, zz in pending.pop(0):
                    sib[step, p].wait_recv()
                    items.append((1 - core, zz))
            add_products(p, items)
        items = []
        for step, zz in sum(pending, []):
            sib[step, p].wait_recv()
            items.append((1 - core, zz))
        add_products(p, items)
        y_copy[p] = projection_part(p)
    some(len(work))
    for p in range(2):
        projection_end(p, y_copy[p])

    for number in (3, 4, 5):
        outgoing[number].wait_send()
    for group in (to_sibling, forwarded, far_copy, near_copy, ag, sib, y_copy):
        for copy in group.values():
            copy.wait_send()


def hand_over(*refs):
    count = (len(refs) - 1) // 2
    sems = refs[-1]
    copies = [pltpu.make_async_copy(refs[k], refs[count + k], sems.at[k]) for k in range(count)]
    for copy in copies:
        copy.start()
    for copy in copies:
        copy.wait()


def solution(mesh):
    zs = mesh.shape["dp"] // 4

    def on_device(act, og, table, plan, ls, rs, lr, rr, wb):
        toks = act.shape[0]
        bs = ls.shape[-1]
        rb = act.shape[1] // bs
        slots = table.shape[1]
        half = bs // 2
        quarter = bs // 4
        mats = [value.reshape(bs, bs) for value in (ls, rs, lr, rr, wb)]
        far = zs // 2
        leaves = [jax.ShapeDtypeStruct((bs, bs), F32)] * 4
        leaves += [jax.ShapeDtypeStruct((bs, bs), BF), jax.ShapeDtypeStruct((toks, CB * bs), BF)]
        vmem = pl.BlockSpec(memory_space=pltpu.VMEM)
        any_space = pl.BlockSpec(memory_space=pl.ANY)
        smem = pl.BlockSpec(memory_space=pltpu.SMEM)
        f_mat = pltpu.VMEM((bs, bs), F32)
        b_mat = pltpu.VMEM((bs, bs), BF)
        dma = pltpu.SemaphoreType.DMA
        outs = pl.pallas_call(
            functools.partial(kernel, zs, toks, rb, bs, slots),
            out_shape=[pltpu.VMEM(leaf.shape, leaf.dtype) for leaf in leaves],
            in_specs=[smem, smem] + [any_space] * 7,
            out_specs=[vmem] * 6,
            scratch_shapes=[
                pltpu.VMEM((rb, 4 * toks, half), BF),
                pltpu.VMEM((rb, 4 * toks, half), BF),
                pltpu.VMEM((CB, 4 * toks, half), BF),
                pltpu.VMEM((CB, 4 * toks, half), BF),
                pltpu.VMEM((2, 2, 2, quarter, half), BF),
                pltpu.VMEM((2, 2, 2, quarter, half), BF),
                pltpu.VMEM((2, far - 1, 2, 2, half, half), BF),
                pltpu.VMEM((2, far - 1, 2, 2, half, half), BF),
                pltpu.VMEM((2, zs, 2, bs, half), BF),
                pltpu.VMEM((CB, 2 * toks, bs), F32),
                pltpu.VMEM((2, CB, toks, half), BF),
                pltpu.VMEM((2, CB, toks, half), BF),
                b_mat,
                b_mat, b_mat, b_mat, b_mat, b_mat, b_mat, b_mat, b_mat,
                pltpu.VMEM((bs, half), F32),
                f_mat, f_mat, f_mat, b_mat, b_mat, b_mat, b_mat, b_mat,
                pltpu.SemaphoreType.REGULAR,
                dma((2 * (CB + rb) + 5,)),
                dma((18,)), dma((18,)),
                dma((2, far, 2, 2)), dma((2, far, 2, 2)),
                dma((2, far, 2, 2)), dma((2, far, 2, 2)),
                dma((zs, 2)), dma((zs, 2)),
                dma((2,)), dma((2,)),
            ],
            compiler_params=pltpu.CompilerParams(
                collective_id=0, has_side_effects=True, vmem_limit_bytes=57 * 1024 * 1024
            ),
        )(table, plan, act, og, *mats)
        outs = pl.pallas_call(
            hand_over,
            out_shape=leaves,
            in_specs=[vmem] * 6,
            out_specs=[any_space] * 6,
            scratch_shapes=[dma((6,))],
            compiler_params=pltpu.CompilerParams(vmem_limit_bytes=4 * 1024 * 1024),
        )(*[pltpu.with_memory_space_constraint(value, pltpu.VMEM) for value in outs])
        return tuple(value.reshape(1, 1, bs, bs) for value in outs[:5]) + (outs[5],)

    block = P("mp", "dp", None, None)
    return jax.shard_map(
        on_device,
        mesh=mesh,
        in_specs=(P("dp", None), P("dp", "mp"), P(), P(), block, block, block, block, block),
        out_specs=(block, block, block, block, block, P("dp", "mp")),
        check_vma=False,
    )
```

time: 135 us -> 126 us (0.933)
  local copies, waits for them, and re-layouts: 8.98 us -> 0 us
    unnamed x16 -> x0, local copies, waits for them, and re-layouts: 8.98 us -> none
    pallas_call x0 -> x1, Pallas kernels: none -> 2.39 us  [on_device(): pl.pallas_call(hand_over, out_shape=leaves, in_specs=[vmem] * 6, out_spec...]
    pallas_call x1, Pallas kernels: 125 us -> 123 us  [on_device(): pl.pallas_call(functools.partial(kernel, zs, toks, rb, bs, slots), out_sh...]
where the time goes in v2:
time: 126 us
  Pallas kernels  125 us (99%)
    pallas_call x1, Pallas kernels, on_device(): pl.pallas_call(functools.partial(kernel, zs, toks, rb, bs, slots), out_sh...  123 us

profile of v2, /device:TPU:1, one launch (start us, length us, event | category | flops | bytes accessed | tf_op | source)
XLA Modules:
  0.0 126.0 jit_solution(11173190460466504781)
XLA Ops:
  0.6 122.8 %shard_map.136 = (f32[512,512]{1,0:T(8,128)S(1)}, f32[512,512]{1,0:T(8,128)S(1)}, f32[512,512]{1,0:T(8,128)S(1)}, f32[512,512]{1,0:T(8,128)S(1)}, bf16[512,512]{...) custom-call(s32[8,32]{1,0:T(8,128)} %table.1, s32[8,7]{1,0:T(8,128)} %plan.1, bf16[128,3584]{1,0:T(8,128)(2,1)} %act.1, ...), custom_call_target="tpu_custom_call" | custom-call | tf_op jit(solution)/shard_map/pallas_call | solution.py:490
  123.5 2.4 %shard_map.137 = (f32[512,512]{1,0:T(8,128)}, f32[512,512]{1,0:T(8,128)}, f32[512,512]{1,0:T(8,128)}, f32[512,512]{1,0:T(8,128)}, bf16[512,512]{1,0:T(8,128)(2,1)}, /*index=5*/bf16[128,2048]{1,0:T(8,128)(2,1)}) custom-call(f32[512,512]{1,0:T(8,128)S(1)} %get-tuple-element.18.refs_0_, f32[512,512]{1,0:T(8,128)S(1)} %get-tuple-element.19.refs_1_, ...), custom_call_target="tpu_custom_call" | custom-call | tf_op jit(solution)/shard_map/pallas_call | solution.py:524

commit v3 on v2

v3 whole, which is shorter than its diff:
```python
import functools

import jax
import jax.numpy as jnp
from jax import lax
from jax.experimental import pallas as pl
from jax.experimental.pallas import tpu as pltpu
from jax.sharding import PartitionSpec as P

BETA = 0.9
STEP = 0.1
EPS = 1e-06
CB = 4

PACE = 3

MESH = pl.DeviceIdType.MESH
BF = jnp.bfloat16
F32 = jnp.float32


def dot(left, right):
    return jnp.dot(left, right, preferred_element_type=F32)


def dot_tn(left, right):
    return lax.dot_general(left, right, (((0,), (0,)), ((), ())), preferred_element_type=F32)


def dot_nt(left, right):
    return lax.dot_general(left, right, (((1,), (1,)), ((), ())), preferred_element_type=F32)


def split(value):
    high = value.astype(BF)
    return high, (value - high.astype(F32)).astype(BF)


def kernel(
    zs, toks, rb, bs, slots,
    table, plan, act, og, ls, rs, lr, rr, wb,
    nl, nr, lold, rold, nw, pout,
    a_0, a_1, a_2, e_0, e_1, far_s, far_r, near_s, near_r, wag_0, wag_1, acc, ysend_0, ysend_1, yrecv_0, yrecv_1,
    wold, mid, lh, ll, rh, rl, gh, gl, th, tl, tf,
    nf, m1f, xf, mb0, mb1, nb, kb, xb,
    load_sem, p0_send, p0_recv, rs_send, rs_recv, ag_send, ag_recv, sib_send, sib_recv, y_ssem, y_rsem,
):
    half = bs // 2
    quarter = bs // 4
    far = zs // 2
    a_parts, e_parts = (a_0, a_1, a_2), (e_0, e_1)
    a_cols = ((0, quarter), (quarter, half), (half, bs))
    wags, ysends, yrecvs = (wag_0, wag_1), (ysend_0, ysend_1), (yrecv_0, yrecv_1)
    chunks = ((0, half), (half, bs))
    nblk = rb * CB
    dp = lax.axis_index("dp")
    mp = lax.axis_index("mp")
    core = lax.rem(dp, 2)
    z = lax.rem(dp // 2, zs)
    y = dp // (2 * zs)

    def device(yy, zz, cc):
        return yy * (2 * zs) + zz * 2 + cc

    up = lax.rem(z + 1, zs)
    down = lax.rem(z + zs - 1, zs)
    ring = ((device(y, up, core), mp), (device(y, down, core), mp))
    sibling = (device(y, z, 1 - core), mp)
    across = (device(1 - y, z, core), mp)
    across_other = (device(1 - y, z, core), mp + 1 - 2 * lax.rem(mp, 2))

    def remote(src, dst, send, recv, to):
        copy = pltpu.make_async_remote_copy(
            src_ref=src, dst_ref=dst, send_sem=send, recv_sem=recv, device_id=to, device_id_type=MESH
        )
        copy.start()
        return copy

    def rows_of(yy, cc):
        return pl.ds(pl.multiple_of((cc * 2 + yy) * toks, toks), toks)

    def local(src, dst, sem):
        copy = pltpu.make_async_copy(src, dst, sem)
        copy.start()
        return copy

    mine = rows_of(y, core)
    loads = {}
    base = 0
    for kind, i in (("e", 0), ("a", 0), ("a", 1), ("e", 1), ("a", 2)):
        source, dst, count = (og, e_parts[i], CB) if kind == "e" else (act, a_parts[i], rb)
        lo, hi = (i * half, (i + 1) * half) if kind == "e" else a_cols[i]
        loads[kind, i] = [
            local(source.at[:, k * bs + lo : k * bs + hi], dst.at[k, mine, :], load_sem.at[base + k]) for k in range(count)
        ]
        base += count
    load_mats = [
        local(src, dst, load_sem.at[base + k])
        for k, (src, dst) in enumerate(((lr, lold), (rr, rold), (wb, wold), (ls, nl), (rs, nr)))
    ]

    barrier = pltpu.get_barrier_semaphore()
    for other in (sibling, across, across_other) + ring:
        pl.semaphore_signal(barrier, inc=1, device_id=other, device_id_type=MESH)
    pl.semaphore_wait(barrier, 5)

    def part(number, rows):
        return (
            e_0.at[:, rows, :],
            a_0.at[:, rows, :],
            e_1.at[:, rows, :],
            a_1.at[:, rows, :],
            a_2.at[rb - 2 : rb, rows, :],
            a_2.at[0 : rb - 2, rows, :],
        )[number]

    parts = 6

    def send_part(number, rows, slot, to):
        ref = part(number, rows)
        return remote(ref, ref, p0_send.at[slot], p0_recv.at[slot], to)

    outgoing = {}
    to_sibling = {}
    forwarded = {}

    def send_parts(numbers, needs):
        for what in needs:
            for copy in loads[what]:
                copy.wait()
        for number in numbers:
            outgoing[number] = send_part(number, mine, number, across_other if number in (1, 3, 5) else across)
        for number in numbers:
            to_sibling[number] = send_part(number, mine, parts + number, sibling)

    def sent(numbers):
        for number in numbers:
            outgoing[number].wait_send()

    send_parts((0, 1), (("e", 0), ("a", 0)))
    sent((0, 1))
    send_parts((2, 3), (("e", 1), ("a", 1)))
    sent((2, 3))
    send_parts((4, 5), (("a", 2),))
    theirs = rows_of(1 - y, core)

    def forward(numbers):
        for number in numbers:
            outgoing[number].wait_recv()
            forwarded[number] = send_part(number, theirs, 2 * parts + number, sibling)

    def have(numbers):
        for number in numbers:
            to_sibling[number].wait_recv()
            forwarded[number].wait_recv()

    def block_at(zz, cc):
        return table[mp, y * (2 * zs) + zz * 2 + cc]

    def row_and_col(block):
        safe = jnp.where(block < nblk, block, 0)
        return safe // CB, lax.rem(safe, CB)

    def partial_grad(zz, piece):
        r, c = row_and_col(block_at(zz, core))
        return dot_tn(a_parts[piece[0]][r], e_parts[piece[1]][c])

    pieces = ((0, 0), (1, 0), (0, 1), (1, 1), (2, 0), (2, 1))
    rs_copy = {}

    def piece_rows(piece, part=None):
        lo, hi = a_cols[piece[0]]
        if part is None:
            return slice(lo, hi)
        middle = (lo + hi) // 2
        return slice(lo, middle) if part == 0 else slice(middle, hi)

    def send_sum(way, level, piece, src, dst):
        n = pieces.index(piece)
        rs_copy[way, level, piece] = remote(src, dst, rs_send.at[way, level, n], rs_recv.at[way, level, n], ring[way])

    def target(way, d):
        return lax.rem(z + d, zs) if way == 0 else lax.rem(z + zs - d, zs)

    def send_start(piece):
        j = piece[1]
        lo, hi = a_cols[piece[0]]
        middle = (hi - lo) // 2
        rows = slice(lo // 2, hi // 2)
        value = partial_grad(target(0, far), piece).astype(BF)
        for way in range(2):
            far_s[way, j, rows, :] = value[way * middle : (way + 1) * middle, :]
            send_sum(way, 0, piece, far_s.at[way, j, rows, :], far_r.at[way, j, rows, :])
        for way in range(2):
            rest = 1 - way
            value = partial_grad(target(way, far - 1), piece)
            rows = piece_rows(piece, rest)
            near_s[way, far - 2, j, rows, :] = value[rest * middle : (rest + 1) * middle, :].astype(BF)
            mid[way, j, lo // 2 : hi // 2, :] = value[way * middle : (way + 1) * middle, :]
            send_sum(way, far, piece, near_s.at[way, far - 2, j, rows, :], near_r.at[way, far - 2, j, rows, :])

    def send_near(d, piece):
        if d < 1:
            return
        j = piece[1]
        lo, hi = a_cols[piece[0]]
        for way in range(2):
            if d == far - 1:
                rows = piece_rows(piece, way)
                value = mid[way, j, lo // 2 : hi // 2, :]
                rs_copy[way, 0, piece].wait_recv()
                value = value + far_r[way, j, lo // 2 : hi // 2, :].astype(F32)
            else:
                rows = piece_rows(piece)
                value = partial_grad(target(way, d), piece)
                rs_copy[way, d + 1, piece].wait_recv()
                if d == far - 2:
                    rs_copy[way, far, piece].wait_recv()
                value = value + near_r[way, d, j, rows, :].astype(F32)
            near_s[way, d - 1, j, rows, :] = value.astype(BF)
            send_sum(way, d, piece, near_s.at[way, d - 1, j, rows, :], near_r.at[way, d - 1, j, rows, :])

    forward((0, 1))
    have((0, 1))
    send_start(pieces[0])
    forward((3,))
    have((3,))
    send_start(pieces[1])
    forward((2,))
    send_near(far - 1, pieces[0])
    have((2,))
    send_start(pieces[2])
    send_start(pieces[3])
    send_near(far - 1, pieces[1])
    send_near(far - 2, pieces[0])
    forward((4, 5))
    have((4, 5))
    send_start(pieces[4])
    send_start(pieces[5])
    send_near(far - 1, pieces[2])
    send_near(far - 1, pieces[3])
    send_near(far - 2, pieces[1])
    send_near(far - 1, pieces[4])
    send_near(far - 1, pieces[5])
    send_near(far - 2, pieces[2])
    send_near(far - 2, pieces[3])
    for copy in load_mats:
        copy.wait()
    lh[...], ll[...] = split(lold[...])
    rh[...], rl[...] = split(rold[...])
    send_near(far - 3, pieces[0])
    send_near(far - 3, pieces[1])
    send_near(far - 2, pieces[4])
    send_near(far - 2, pieces[5])
    for n in (2, 3, 4, 5):
        send_near(far - 3, pieces[n])
    own_block = block_at(z, core)
    filled = jnp.where(own_block < nblk, 1.0, 0.0).astype(F32)

    def sum_piece(piece):
        j = piece[1]
        rows = piece_rows(piece)
        cols = slice(j * half, (j + 1) * half)
        value = partial_grad(z, piece)
        for way in range(2):
            rs_copy[way, 1, piece].wait_recv()
            if far == 2:
                rs_copy[way, far, piece].wait_recv()
        value = (value + near_r[0, 0, j, rows, :].astype(F32) + near_r[1, 0, j, rows, :].astype(F32)) * filled
        gh[rows, cols], gl[rows, cols] = split(value)

    def left_term(i, j):
        rows, cols = slice(i * half, (i + 1) * half), slice(j * half, (j + 1) * half)
        return dot(lh[:, rows], gh[rows, cols]) + dot(lh[:, rows], gl[rows, cols]) + dot(ll[:, rows], gh[rows, cols])

    def right_term(j, lo, hi):
        rows = slice(j * half, (j + 1) * half)
        return dot(th[:, rows], rh[rows, lo:hi]) + dot(th[:, rows], rl[rows, lo:hi]) + dot(tl[:, rows], rh[rows, lo:hi])

    lefts = []
    for j in range(2):
        sum_piece((0, j))
        sum_piece((1, j))
        lefts.append(left_term(0, j))
    for j in range(2):
        sum_piece((2, j))
        cols = slice(j * half, (j + 1) * half)
        th[:, cols], tl[:, cols] = split(lefts[j] + left_term(1, j))
        if j == 0:
            tf[...] = right_term(0, *chunks[0])

    ag = {}
    sib = {}

    def piece(cc, zz, p, k):
        return wags[p].at[cc, zz, k * half : (k + 1) * half, :]

    def send_ring(way, zz, d, p, k):
        ref = piece(core, zz, p, k)
        ag[way, d, p, k] = remote(ref, ref, ag_send.at[way, d - 1, p, k], ag_recv.at[way, d - 1, p, k], ring[way])

    def send_sibling(zz, step, p):
        ref = wags[p].at[core, zz]
        sib[step, p] = remote(ref, ref, sib_send.at[step, p], sib_recv.at[step, p], sibling)

    def reach(way, k):
        return far if way == k else far - 1

    def behind(way, d):
        return lax.rem(z + zs - d, zs) if way == 0 else lax.rem(z + d, zs)

    def make_weights(p):
        lo, hi = chunks[p]
        update = (tf[...] if p == 0 else right_term(0, lo, hi)) + right_term(1, lo, hi)
        value = (wold[:, lo:hi].astype(F32) - STEP * update).astype(BF)
        wags[p][core, z] = value
        nw[:, lo:hi] = value

    def send_own(p, k):
        for way in range(2):
            send_ring(way, z, 1, p, k if way == 0 else 1 - k)

    def add_products(p, items):
        lo, hi = chunks[p]
        terms = []
        for cc, zz in items:
            block = block_at(zz, cc)
            r, c = row_and_col(block)
            rows = pl.ds(pl.multiple_of(core * (2 * toks), 2 * toks), 2 * toks)
            lhs = jnp.concatenate([a_0[r, rows, :], a_1[r, rows, :]], axis=1)
            term = dot(lhs, wags[p][cc, zz, 0:half, :]) + dot(a_2[r, rows, :], wags[p][cc, zz, half:bs, :])
            terms.append((block, c, term))
        for col in range(CB):
            value = acc[col, :, lo:hi]
            for block, c, term in terms:
                weight = jnp.where((block < nblk) & (c == col), 1.0, 0.0).astype(F32)
                value = value + term * weight
            acc[col, :, lo:hi] = value

    own_flag = jnp.zeros((), jnp.int32)
    for k in range(plan.shape[1]):
        own_flag = jnp.where(plan[mp, k] == own_block, 1, own_flag)
    own_flag = jnp.where(own_block < nblk, own_flag, 0)

    def new_left():
        nl[...] = BETA * nl[...] + dot_nt(gh[...], gh[...]) + dot_nt(gh[...], gl[...]) + dot_nt(gl[...], gh[...])

    def new_right():
        nr[...] = BETA * nr[...] + dot_tn(gh[...], gh[...]) + dot_tn(gh[...], gl[...]) + dot_tn(gl[...], gh[...])

    width = half

    def eye_tile(lo):
        rows = lax.broadcasted_iota(jnp.int32, (bs, width), 0)
        cols = lax.broadcasted_iota(jnp.int32, (bs, width), 1) + lo
        return jnp.where(rows == cols, 1.0, 0.0).astype(F32)

    def tiles(body):
        for lo in range(0, bs, width):
            body(slice(lo, lo + width), lo)

    def newton(stats, old):
        scale = {}

        def start():
            total = jnp.sum(stats[...] * stats[...], axis=(0, 1), keepdims=True)
            scale["z"] = 5.0 / (2.0 * jnp.sqrt(total + EPS))
            scale["root"] = jnp.sqrt(jnp.sqrt(scale["z"]))
            mb0[...] = (scale["z"] * stats[...]).astype(BF)

            def body(cols, lo):
                value = (-0.625 * scale["z"]) * stats[:, cols] + 0.0625 * dot(mb0[...], mb0[:, cols])
                nf[:, cols] = value
                nb[:, cols] = value.astype(BF)

            tiles(body)

        def fourth_power():
            def body(cols, lo):
                kb[:, cols] = (3.125 * nf[:, cols] + dot(nb[...], nb[:, cols])).astype(BF)

            tiles(body)

        def first_coupled():
            def body(cols, lo):
                value = (2.44140625 * scale["z"]) * stats[:, cols] + dot(kb[...], mb0[:, cols])
                m1f[:, cols] = value
                mb1[:, cols] = value.astype(BF)

            tiles(body)

        def second_iterate():
            def body(cols, lo):
                value = 1.5625 * eye_tile(lo) - 0.3125 * (scale["z"] * stats[:, cols] + m1f[:, cols])
                value = scale["root"] * (value + 0.0625 * dot(mb0[...], mb1[:, cols]))
                xf[:, cols] = value
                xb[:, cols] = value.astype(BF)

            tiles(body)

        def second_square():
            def body(cols, lo):
                value = -0.625 * m1f[:, cols] + 0.0625 * dot(mb1[...], mb1[:, cols])
                nf[:, cols] = value
                nb[:, cols] = value.astype(BF)

            tiles(body)

        def second_coupled():
            def body(cols, lo):
                mb0[:, cols] = (2.44140625 * m1f[:, cols] + dot(kb[...], mb1[:, cols])).astype(BF)

            tiles(body)

        def finish():
            mask = jnp.full((bs, width), own_flag, jnp.int32) > 0

            def body(cols, lo):
                value = 1.25 * xf[:, cols] - 0.25 * dot(xb[...], mb0[:, cols])
                old[:, cols] = jnp.where(mask, value, old[:, cols])

            tiles(body)

        return [start, fourth_power, first_coupled, second_iterate, second_square, fourth_power, second_coupled, finish]

    work = [new_left, new_right] + newton(nl, lold) + newton(nr, rold)

    def some(count):
        for _ in range(count):
            if work:
                work.pop(0)()

    def projection_part(p):
        other = pl.ds(pl.multiple_of((1 - y) * toks, toks), toks)
        ysends[p][...] = acc[:, other, chunks[p][0] : chunks[p][1]].astype(BF)
        return remote(ysends[p], yrecvs[p], y_ssem.at[p], y_rsem.at[p], across)

    def projection_end(p, copy):
        copy.wait_recv()
        own = pl.ds(pl.multiple_of(y * toks, toks), toks)
        lo, hi = chunks[p]
        value = acc[:, own, lo:hi] + yrecvs[p][...].astype(F32)
        for col in range(CB):
            pout[:, col * bs + lo : col * bs + hi] = value[col].astype(BF)

    y_copy = {}
    sib_steps = [1, 1]
    ready = []
    later = []

    def compute(count):
        for _ in range(count):
            if ready:
                ready.pop(0)()
            else:
                some(1)
        ready.extend(later)
        later.clear()

    def sibling_products(p, items):
        for step, _ in items:
            sib[step, p].wait_recv()
        add_products(p, [(1 - core, zz) for _, zz in items])

    def finish_chunk(p):
        y_copy[p] = projection_part(p)

    def receive(p, d, k):
        for way in range(2):
            order = k if way == 0 else 1 - k
            if d <= reach(way, order):
                ag[way, d, p, order].wait_recv()
                if d < reach(way, order):
                    send_ring(way, behind(way, d), d + 1, p, order)
        if k == 1 or d == far:
            arrived = [behind(0, d), behind(1, d)] if d < far else [behind(0, d)]
            fresh = []
            for zz in arrived:
                send_sibling(zz, sib_steps[p], p)
                fresh.append((sib_steps[p], zz))
                sib_steps[p] += 1
            ready.append(functools.partial(add_products, p, [(core, zz) for zz in arrived]))
            later.append(functools.partial(sibling_products, p, fresh))
            if d == far:
                later.append(functools.partial(finish_chunk, p))

    make_weights(0)
    send_own(0, 0)
    send_own(0, 1)
    send_sibling(z, 0, 0)
    make_weights(1)
    send_own(1, 0)
    send_sibling(z, 0, 1)
    acc[...] = jnp.zeros_like(acc)
    ready.append(functools.partial(add_products, 0, [(core, z)]))
    later.append(functools.partial(sibling_products, 0, [(0, z)]))
    compute(2)
    for d in range(1, far + 1):
        for k in range(2 if d < far else 1):
            receive(0, d, k)
            if d == 1 and k == 1:
                send_own(1, 1)
            compute(PACE)
            if (d, k) == (max(far - 2, 1), 1):
                receive(1, 1, 0)
                ready.append(functools.partial(add_products, 1, [(core, z)]))
                later.append(functools.partial(sibling_products, 1, [(0, z)]))
                compute(PACE)
            if (d, k) == (far - 1, 1):
                receive(1, 1, 1)
                compute(PACE)
    for d in range(2, far + 1):
        for k in range(2 if d < far else 1):
            receive(1, d, k)
            compute(PACE if d < far else 1)
    while ready:
        ready.pop(0)()
    some(len(work))
    for p in range(2):
        projection_end(p, y_copy[p])

    sent((4, 5))
    for group in (to_sibling, forwarded, rs_copy, ag, sib, y_copy):
        for copy in group.values():
            copy.wait_send()


def hand_over(*refs):
    count = (len(refs) - 1) // 2
    sems = refs[-1]
    copies = [pltpu.make_async_copy(refs[k], refs[count + k], sems.at[k]) for k in range(count)]
    for copy in copies:
        copy.start()
    for copy in copies:
        copy.wait()


def solution(mesh):
    zs = mesh.shape["dp"] // 4

    def on_device(act, og, table, plan, ls, rs, lr, rr, wb):
        toks = act.shape[0]
        bs = ls.shape[-1]
        rb = act.shape[1] // bs
        slots = table.shape[1]
        half = bs // 2
        quarter = bs // 4
        mats = [value.reshape(bs, bs) for value in (ls, rs, lr, rr, wb)]
        far = zs // 2
        leaves = [jax.ShapeDtypeStruct((bs, bs), F32)] * 4
        leaves += [jax.ShapeDtypeStruct((bs, bs), BF), jax.ShapeDtypeStruct((toks, CB * bs), BF)]
        vmem = pl.BlockSpec(memory_space=pltpu.VMEM)
        any_space = pl.BlockSpec(memory_space=pl.ANY)
        smem = pl.BlockSpec(memory_space=pltpu.SMEM)
        f_mat = pltpu.VMEM((bs, bs), F32)
        b_mat = pltpu.VMEM((bs, bs), BF)
        dma = pltpu.SemaphoreType.DMA
        outs = pl.pallas_call(
            functools.partial(kernel, zs, toks, rb, bs, slots),
            out_shape=[pltpu.VMEM(leaf.shape, leaf.dtype) for leaf in leaves],
            in_specs=[smem, smem] + [any_space] * 7,
            out_specs=[vmem] * 6,
            scratch_shapes=[
                pltpu.VMEM((rb, 4 * toks, quarter), BF),
                pltpu.VMEM((rb, 4 * toks, quarter), BF),
                pltpu.VMEM((rb, 4 * toks, half), BF),
                pltpu.VMEM((CB, 4 * toks, half), BF),
                pltpu.VMEM((CB, 4 * toks, half), BF),
                pltpu.VMEM((2, 2, half, half), BF),
                pltpu.VMEM((2, 2, half, half), BF),
                pltpu.VMEM((2, far - 1, 2, bs, half), BF),
                pltpu.VMEM((2, far - 1, 2, bs, half), BF),
                pltpu.VMEM((2, zs, bs, half), BF),
                pltpu.VMEM((2, zs, bs, half), BF),
                pltpu.VMEM((CB, 2 * toks, bs), F32),
                pltpu.VMEM((CB, toks, half), BF),
                pltpu.VMEM((CB, toks, half), BF),
                pltpu.VMEM((CB, toks, half), BF),
                pltpu.VMEM((CB, toks, half), BF),
                b_mat,
                pltpu.VMEM((2, 2, half, half), F32),
                b_mat, b_mat, b_mat, b_mat, b_mat, b_mat, b_mat, b_mat,
                pltpu.VMEM((bs, half), F32),
                f_mat, f_mat, f_mat, b_mat, b_mat, b_mat, b_mat, b_mat,
                dma((2 * CB + 3 * rb + 5,)),
                dma((18,)), dma((18,)),
                dma((2, far + 1, 6)), dma((2, far + 1, 6)),
                dma((2, far, 2, 2)), dma((2, far, 2, 2)),
                dma((zs, 2)), dma((zs, 2)),
                dma((2,)), dma((2,)),
            ],
            compiler_params=pltpu.CompilerParams(
                collective_id=0, has_side_effects=True, vmem_limit_bytes=57 * 1024 * 1024
            ),
        )(table, plan, act, og, *mats)
        outs = pl.pallas_call(
            hand_over,
            out_shape=leaves,
            in_specs=[vmem] * 6,
            out_specs=[any_space] * 6,
            scratch_shapes=[dma((6,))],
            compiler_params=pltpu.CompilerParams(vmem_limit_bytes=4 * 1024 * 1024),
        )(*[pltpu.with_memory_space_constraint(value, pltpu.VMEM) for value in outs])
        return tuple(value.reshape(1, 1, bs, bs) for value in outs[:5]) + (outs[5],)

    block = P("mp", "dp", None, None)
    return jax.shard_map(
        on_device,
        mesh=mesh,
        in_specs=(P("dp", None), P("dp", "mp"), P(), P(), block, block, block, block, block),
        out_specs=(block, block, block, block, block, P("dp", "mp")),
        check_vma=False,
    )
```

time: 126 us -> 124 us (0.984)
  Pallas kernels: 125 us -> 123 us
    pallas_call x1, Pallas kernels: 123 us -> 120 us  [on_device(): pl.pallas_call(functools.partial(kernel, zs, toks, rb, bs, slots), out_sh...]
where the time goes in v3:
time: 124 us
  Pallas kernels  123 us (99%)
    pallas_call x1, Pallas kernels, on_device(): pl.pallas_call(functools.partial(kernel, zs, toks, rb, bs, slots), out_sh...  120 us

profile of v3, /device:TPU:1, one launch (start us, length us, event | category | flops | bytes accessed | tf_op | source)
XLA Modules:
  0.0 123.7 jit_solution(4143559486078164170)
XLA Ops:
  0.6 120.5 %shard_map.136 = (f32[512,512]{1,0:T(8,128)S(1)}, f32[512,512]{1,0:T(8,128)S(1)}, f32[512,512]{1,0:T(8,128)S(1)}, f32[512,512]{1,0:T(8,128)S(1)}, bf16[512,512]{...) custom-call(s32[8,32]{1,0:T(8,128)} %table.1, s32[8,7]{1,0:T(8,128)} %plan.1, bf16[128,3584]{1,0:T(8,128)(2,1)} %act.1, ...), custom_call_target="tpu_custom_call" | custom-call | tf_op jit(solution)/shard_map/pallas_call | solution.py:558
  121.1 2.4 %shard_map.137 = (f32[512,512]{1,0:T(8,128)}, f32[512,512]{1,0:T(8,128)}, f32[512,512]{1,0:T(8,128)}, f32[512,512]{1,0:T(8,128)}, bf16[512,512]{1,0:T(8,128)(2,1)}, /*index=5*/bf16[128,2048]{1,0:T(8,128)(2,1)}) custom-call(f32[512,512]{1,0:T(8,128)S(1)} %get-tuple-element.18.refs_0_, f32[512,512]{1,0:T(8,128)S(1)} %get-tuple-element.19.refs_1_, ...), custom_call_target="tpu_custom_call" | custom-call | tf_op jit(solution)/shard_map/pallas_call | solution.py:596

commit v4 on v3

--- a/solution.py
+++ b/solution.py
@@ -13,6 +13,7 @@
 CB = 4
 
 PACE = 3
+SIBLING_LAG = 4
 
 MESH = pl.DeviceIdType.MESH
 BF = jnp.bfloat16
@@ -43,7 +44,7 @@
     a_0, a_1, a_2, e_0, e_1, far_s, far_r, near_s, near_r, wag_0, wag_1, acc, ysend_0, ysend_1, yrecv_0, yrecv_1,
     wold, mid, lh, ll, rh, rl, gh, gl, th, tl, tf,
     nf, m1f, xf, mb0, mb1, nb, kb, xb,
-    load_sem, p0_send, p0_recv, rs_send, rs_recv, ag_send, ag_recv, sib_send, sib_recv, y_ssem, y_rsem,
+    gate, load_sem, p0_send, p0_recv, rs_send, rs_recv, ag_send, ag_recv, sib_send, sib_recv, y_ssem, y_rsem,
 ):
     half = bs // 2
     quarter = bs // 4
@@ -250,10 +251,22 @@
     rh[...], rl[...] = split(rold[...])
     send_near(far - 3, pieces[0])
     send_near(far - 3, pieces[1])
+
+    @pl.when(core == 1)
+    def _():
+        pl.semaphore_wait(gate, 1)
+
     send_near(far - 2, pieces[4])
     send_near(far - 2, pieces[5])
-    for n in (2, 3, 4, 5):
-        send_near(far - 3, pieces[n])
+    send_near(far - 3, pieces[2])
+    send_near(far - 3, pieces[3])
+    send_near(far - 3, pieces[4])
+    send_near(far - 3, pieces[5])
+
+    @pl.when(core == 0)
+    def _():
+        pl.semaphore_signal(gate, inc=1, device_id=sibling, device_id_type=MESH)
+
     own_block = block_at(z, core)
     filled = jnp.where(own_block < nblk, 1.0, 0.0).astype(F32)
 
@@ -454,8 +467,10 @@
                 ready.pop(0)()
             else:
                 some(1)
-        ready.extend(later)
-        later.clear()
+        for entry in later:
+            entry[0] -= 1
+        while later and later[0][0] <= 0:
+            ready.append(later.pop(0)[1])
 
     def sibling_products(p, items):
         for step, _ in items:
@@ -480,9 +495,9 @@
                 fresh.append((sib_steps[p], zz))
                 sib_steps[p] += 1
             ready.append(functools.partial(add_products, p, [(core, zz) for zz in arrived]))
-            later.append(functools.partial(sibling_products, p, fresh))
+            later.append([SIBLING_LAG, functools.partial(sibling_products, p, fresh)])
             if d == far:
-                later.append(functools.partial(finish_chunk, p))
+                later.append([SIBLING_LAG, functools.partial(finish_chunk, p)])
 
     make_weights(0)
     send_own(0, 0)
@@ -493,7 +508,7 @@
     send_sibling(z, 0, 1)
     acc[...] = jnp.zeros_like(acc)
     ready.append(functools.partial(add_products, 0, [(core, z)]))
-    later.append(functools.partial(sibling_products, 0, [(0, z)]))
+    later.append([SIBLING_LAG, functools.partial(sibling_products, 0, [(0, z)])])
     compute(2)
     for d in range(1, far + 1):
         for k in range(2 if d < far else 1):
@@ -504,7 +519,7 @@
             if (d, k) == (max(far - 2, 1), 1):
                 receive(1, 1, 0)
                 ready.append(functools.partial(add_products, 1, [(core, z)]))
-                later.append(functools.partial(sibling_products, 1, [(0, z)]))
+                later.append([SIBLING_LAG, functools.partial(sibling_products, 1, [(0, z)])])
                 compute(PACE)
             if (d, k) == (far - 1, 1):
                 receive(1, 1, 1)
@@ -513,6 +528,7 @@
         for k in range(2 if d < far else 1):
             receive(1, d, k)
             compute(PACE if d < far else 1)
+    ready.extend(entry[1] for entry in later)
     while ready:
         ready.pop(0)()
     some(len(work))
@@ -582,6 +598,7 @@
                 b_mat, b_mat, b_mat, b_mat, b_mat, b_mat, b_mat, b_mat,
                 pltpu.VMEM((bs, half), F32),
                 f_mat, f_mat, f_mat, b_mat, b_mat, b_mat, b_mat, b_mat,
+                pltpu.SemaphoreType.REGULAR,
                 dma((2 * CB + 3 * rb + 5,)),
                 dma((18,)), dma((18,)),
                 dma((2, far + 1, 6)), dma((2, far + 1, 6)),

time: 124 us -> 121 us (0.976)
  Pallas kernels: 123 us -> 120 us
    pallas_call x1, Pallas kernels: 120 us -> 117 us  [on_device(): pl.pallas_call(functools.partial(kernel, zs, toks, rb, bs, slots), out_sh...]
where the time goes in v4:
time: 121 us
  Pallas kernels  120 us (99%)
    pallas_call x1, Pallas kernels, on_device(): pl.pallas_call(functools.partial(kernel, zs, toks, rb, bs, slots), out_sh...  117 us

profile of v4, /device:TPU:1, one launch (start us, length us, event | category | flops | bytes accessed | tf_op | source)
XLA Modules:
  0.0 120.6 jit_solution(1905047220677114488)
XLA Ops:
  0.6 117.4 %shard_map.136 = (f32[512,512]{1,0:T(8,128)S(1)}, f32[512,512]{1,0:T(8,128)S(1)}, f32[512,512]{1,0:T(8,128)S(1)}, f32[512,512]{1,0:T(8,128)S(1)}, bf16[512,512]{...) custom-call(s32[8,32]{1,0:T(8,128)} %table.1, s32[8,7]{1,0:T(8,128)} %plan.1, bf16[128,3584]{1,0:T(8,128)(2,1)} %act.1, ...), custom_call_target="tpu_custom_call" | custom-call | tf_op jit(solution)/shard_map/pallas_call | solution.py:574
  118.1 2.4 %shard_map.137 = (f32[512,512]{1,0:T(8,128)}, f32[512,512]{1,0:T(8,128)}, f32[512,512]{1,0:T(8,128)}, f32[512,512]{1,0:T(8,128)}, bf16[512,512]{1,0:T(8,128)(2,1)}, /*index=5*/bf16[128,2048]{1,0:T(8,128)(2,1)}) custom-call(f32[512,512]{1,0:T(8,128)S(1)} %get-tuple-element.18.refs_0_, f32[512,512]{1,0:T(8,128)S(1)} %get-tuple-element.19.refs_1_, ...), custom_call_target="tpu_custom_call" | custom-call | tf_op jit(solution)/shard_map/pallas_call | solution.py:613

commit v5 on v4

--- a/solution.py
+++ b/solution.py
@@ -13,7 +13,7 @@
 CB = 4
 
 PACE = 3
-SIBLING_LAG = 4
+SIBLING_LAG = 2
 
 MESH = pl.DeviceIdType.MESH
 BF = jnp.bfloat16

time: 121 us -> 119 us (0.983)
  Pallas kernels: 120 us -> 118 us
    pallas_call x1, Pallas kernels: 117 us -> 116 us  [on_device(): pl.pallas_call(functools.partial(kernel, zs, toks, rb, bs, slots), out_sh...]
where the time goes in v5:
time: 119 us
  Pallas kernels  118 us (99%)
    pallas_call x1, Pallas kernels, on_device(): pl.pallas_call(functools.partial(kernel, zs, toks, rb, bs, slots), out_sh...  116 us
    pallas_call x1, Pallas kernels, on_device(): pl.pallas_call(hand_over, out_shape=leaves, in_specs=[vmem] * 6, out_spec...  2.39 us

profile of v5, /device:TPU:1, one launch (start us, length us, event | category | flops | bytes accessed | tf_op | source)
XLA Modules:
  0.0 118.9 jit_solution(9481456509493185684)
XLA Ops:
  0.6 115.7 %shard_map.136 = (f32[512,512]{1,0:T(8,128)S(1)}, f32[512,512]{1,0:T(8,128)S(1)}, f32[512,512]{1,0:T(8,128)S(1)}, f32[512,512]{1,0:T(8,128)S(1)}, bf16[512,512]{...) custom-call(s32[8,32]{1,0:T(8,128)} %table.1, s32[8,7]{1,0:T(8,128)} %plan.1, bf16[128,3584]{1,0:T(8,128)(2,1)} %act.1, ...), custom_call_target="tpu_custom_call" | custom-call | tf_op jit(solution)/shard_map/pallas_call | solution.py:574
  116.3 2.4 %shard_map.137 = (f32[512,512]{1,0:T(8,128)}, f32[512,512]{1,0:T(8,128)}, f32[512,512]{1,0:T(8,128)}, f32[512,512]{1,0:T(8,128)}, bf16[512,512]{1,0:T(8,128)(2,1)}, /*index=5*/bf16[128,2048]{1,0:T(8,128)(2,1)}) custom-call(f32[512,512]{1,0:T(8,128)S(1)} %get-tuple-element.18.refs_0_, f32[512,512]{1,0:T(8,128)S(1)} %get-tuple-element.19.refs_1_, ...), custom_call_target="tpu_custom_call" | custom-call | tf_op jit(solution)/shard_map/pallas_call | solution.py:613
